TPU v7x, 512 devices: a whole 4x8x8 slice. The times are simulated.
512 devices in a mesh: gy: 4 (over z_hi, core), gx: 4 (over z_lo), dp: 32 (over x, y).
Axes of the slice: x: 4, y: 8, z: 8 (z_hi: 2, z_lo: 4; z = z_hi * 4 + z_lo), core: 2. Of those that a mesh axis runs over, the one named last changes fastest.
Arguments:
- tokens: bfloat16 [32, 4, 4, 128, 512], P('dp', 'gy', 'gx'), may hold values from -6 to 6
- tile_ids: int32 [32, 4, 4, 2], P('dp'), may hold values from -1 to 15, as said below
- w_qkv: bfloat16 [512, 768], P('dp'), may hold values from -0.25 to 0.25
- w_out: bfloat16 [256, 512], P('dp'), may hold values from -0.75 to 0.75
- norm_gain: float32 [512], replicated, may hold values from 0.1 to 1.9
- rel_bias: float32 [8, 49], replicated, may hold values from -2 to 304
- update_grad: bfloat16 [32, 4, 4, 128, 512], P('dp', 'gy', 'gx'), may hold values from -6 to 6
Outputs:
- update: bfloat16 [32, 4, 4, 128, 512], P('dp', 'gy', 'gx')
- grad_tokens: bfloat16 [32, 4, 4, 128, 512], P('dp', 'gy', 'gx')
- grad_qkv: float32 [512, 768], P('dp')
- grad_out: float32 [256, 512], P('dp')
- grad_gain: float32 [512], replicated
- grad_bias: float32 [8, 49], replicated
Inputs may be any that keep to these rules, and one draw needn't show every extreme that they name: `tile_ids`: for each crop and device the slots first hold distinct tiles of that device's region, numbered row by row with 4 to a row, then -1; each device lists exactly 2 tiles, so no slot holds -1.
All inputs are finite; a program needn't handle non-finite values.
Results may differ from a plain program's by a relative error of at most 0.027.
Values may be sent and summed in bfloat16 or wider, within the bound.
No kernel may reach another device: no remote copies, remote signals or barrier semaphores. Data moves between devices by JAX's collectives and lax.ppermute only.
A program may use at most 64 MiB of HBM per device.

v0:
```python
import jax
import jax.numpy as jnp
from jax import lax
from jax.sharding import PartitionSpec as P

D = 512
HEADS = 8
HD = 32
INNER = 256
TILE = 8
WIN = 7
HALO = 3
REG = 4
SIDE = 32
CAP = 2
ROWS = 128


def padded_2(array, sides, width):
    for axis, dim in sides:
        size, length = (lax.axis_size(axis), array.shape[dim])
        up = [(i, (i + 1) % size) for i in range(size - 1)]
        down = [(j, i) for i, j in up]
        last = lax.slice_in_dim(array, length - width, length, axis=dim)
        first = lax.slice_in_dim(array, 0, width, axis=dim)
        before = lax.ppermute(last, axis, up)
        after = lax.ppermute(first, axis, down)
        array = jnp.concatenate([before, array, after], axis=dim)
    return array


def window_tables():
    win_side = TILE + 2 * HALO
    query_cells = jnp.arange(TILE * TILE, dtype=jnp.int32)
    window_cells = jnp.arange(win_side * win_side, dtype=jnp.int32)
    row_step = (window_cells // win_side)[None, :] - HALO - (query_cells // TILE)[:, None]
    col_step = (window_cells % win_side)[None, :] - HALO - (query_cells % TILE)[:, None]
    inside = (jnp.abs(row_step) <= HALO) & (jnp.abs(col_step) <= HALO)
    offset = (row_step + HALO) * WIN + col_step + HALO
    onehot = (
        (offset[None, :, :] == jnp.arange(WIN * WIN, dtype=jnp.int32)[:, None, None])
        & inside[None, :, :]
    ).astype(jnp.float32)
    return (inside, onehot)


def softmax_scores(queries, key_rows, bias_table, allowed):
    scores = (
        jnp.einsum("nqhd,nkhd->nhqk", queries, key_rows, preferred_element_type=jnp.float32)
        * HD ** (-0.5)
        + bias_table[None]
    )
    scores = jnp.where(allowed, scores, -jnp.inf)
    row_max = jnp.max(scores, axis=-1, keepdims=True)
    exponent = jnp.exp(scores - row_max)
    return exponent / jnp.sum(exponent, axis=-1, keepdims=True)


def shards(tokens, tile_ids, w_qkv, w_out, norm_gain, rel_bias, update_grad):
    grid_high = lax.axis_size("gy")
    grid_wide = lax.axis_size("gx")
    my_row = lax.axis_index("gy")
    my_col = lax.axis_index("gx")
    win_side = TILE + 2 * HALO
    win_cells = win_side * win_side
    padded = SIDE + 2 * HALO
    block_slots = CAP
    block_count = CAP // block_slots
    inside, onehot = window_tables()
    bias_table = jnp.einsum("ho,oqk->hqk", rel_bias, onehot, precision=lax.Precision.HIGHEST)
    w_qkv_all, w_out_all = (
        lax.all_gather(w_qkv, "dp", axis=0, tiled=True),
        lax.all_gather(w_out, "dp", axis=0, tiled=True),
    )
    features = tokens.reshape(ROWS, D).astype(jnp.float32)
    inv_rms = lax.rsqrt(jnp.mean(features * features, axis=-1, keepdims=True) + 1e-06)
    normed = (features * inv_rms * norm_gain).astype(jnp.bfloat16)
    qkv_rows = jnp.dot(normed, w_qkv_all, preferred_element_type=jnp.float32).astype(jnp.bfloat16)
    crop_tiles = tile_ids.reshape(grid_high, grid_wide, CAP)
    slot_tiles = crop_tiles[my_row, my_col]
    is_active = slot_tiles >= 0
    tile_index = jnp.where(is_active, slot_tiles, 0)
    spare_local = REG * REG
    kv_tiles = qkv_rows[:, INNER:].reshape(CAP, TILE * TILE, 2 * INNER)
    tile_grid = (
        jnp.zeros((spare_local + 1, TILE * TILE, 2 * INNER), jnp.bfloat16)
        .at[jnp.where(is_active, slot_tiles, spare_local)]
        .set(kv_tiles)[:spare_local]
    )
    kv_region = (
        tile_grid.reshape(REG, REG, TILE, TILE, 2 * INNER)
        .transpose(0, 2, 1, 3, 4)
        .reshape(SIDE, SIDE, 2 * INNER)
    )
    kv_padded = padded_2(kv_region, (("gy", 0), ("gx", 1)), HALO)
    spare_tile = grid_high * REG * grid_wide * REG
    row_of_dev = jnp.arange(grid_high, dtype=jnp.int32)[:, None, None]
    col_of_dev = jnp.arange(grid_wide, dtype=jnp.int32)[None, :, None]
    flat_tiles = jnp.where(
        crop_tiles >= 0,
        (row_of_dev * REG + crop_tiles // REG) * (grid_wide * REG)
        + col_of_dev * REG
        + crop_tiles % REG,
        spare_tile,
    )
    crop_active = (
        jnp.zeros((spare_tile + 1,), jnp.float32)
        .at[flat_tiles.reshape(-1)]
        .set(1.0)[:spare_tile]
        .reshape(grid_high * REG, grid_wide * REG)
    )
    crop_active = jnp.pad(crop_active, 1)
    nearby = lax.dynamic_slice(crop_active, (my_row * REG, my_col * REG), (REG + 2, REG + 2))
    near_cells = jnp.repeat(jnp.repeat(nearby, TILE, axis=0), TILE, axis=1)
    key_active = (
        near_cells[TILE - HALO : TILE - HALO + padded, TILE - HALO : TILE - HALO + padded] > 0.5
    )
    start_rows = tile_index // REG * TILE
    start_cols = tile_index % REG * TILE
    zero_index = jnp.zeros((), jnp.int32)
    kv_windows = jax.vmap(
        lambda first_row, first_col: lax.dynamic_slice(
            kv_padded, (first_row, first_col, zero_index), (win_side, win_side, 2 * INNER)
        )
    )(start_rows, start_cols).reshape(CAP, win_cells, 2 * INNER)
    key_windows = jax.vmap(
        lambda first_row, first_col: lax.dynamic_slice(
            key_active, (first_row, first_col), (win_side, win_side)
        )
    )(start_rows, start_cols).reshape(CAP, win_cells)
    queries = qkv_rows[:, :INNER].reshape(block_count, block_slots, TILE * TILE, HEADS, HD)
    key_rows = kv_windows[:, :, :INNER].reshape(block_count, block_slots, win_cells, HEADS, HD)
    values = kv_windows[:, :, INNER:].reshape(block_count, block_slots, win_cells, HEADS, HD)
    allowed = (
        inside[None, None] & (key_windows[:, None, None, :] | ~is_active[:, None, None, None])
    ).reshape(block_count, block_slots, 1, TILE * TILE, win_cells)
    live = is_active.astype(jnp.float32).reshape(block_count, block_slots)

    def block_forward(block_items):
        query_block, key_block, value_block, allow_block, live_block = block_items
        attn_probs = softmax_scores(query_block, key_block, bias_table, allow_block)
        probs_bf = attn_probs.astype(jnp.bfloat16)
        attended = jnp.einsum(
            "nhqk,nkhd->nqhd", probs_bf, value_block, preferred_element_type=jnp.float32
        )
        return (attended * live_block[:, None, None, None]).astype(jnp.bfloat16)

    attended = lax.map(block_forward, (queries, key_rows, values, allowed, live)).reshape(
        ROWS, INNER
    )
    update = jnp.dot(attended, w_out_all, preferred_element_type=jnp.float32).astype(jnp.bfloat16)
    row_active = jnp.repeat(is_active, TILE * TILE)
    grad_rows = jnp.where(
        row_active[:, None], update_grad.reshape(ROWS, D), jnp.zeros((), jnp.bfloat16)
    )
    grad_attended = lax.dot_general(
        grad_rows, w_out_all, (((1,), (1,)), ((), ())), preferred_element_type=jnp.float32
    ).astype(jnp.bfloat16)
    grad_out_local = lax.dot_general(
        attended, grad_rows, (((0,), (0,)), ((), ())), preferred_element_type=jnp.float32
    )
    grad_heads = grad_attended.reshape(block_count, block_slots, TILE * TILE, HEADS, HD)

    def block_backward(block_items):
        query_block, key_block, value_block, allow_block, grad_block = block_items
        attn_probs = softmax_scores(query_block, key_block, bias_table, allow_block)
        probs_bf = attn_probs.astype(jnp.bfloat16)
        d_probs = jnp.einsum(
            "nqhd,nkhd->nhqk", grad_block, value_block, preferred_element_type=jnp.float32
        )
        row_delta = jnp.sum(attn_probs * d_probs, axis=-1, keepdims=True)
        d_scores = (attn_probs * (d_probs - row_delta)).astype(jnp.bfloat16)
        d_queries = jnp.einsum(
            "nhqk,nkhd->nqhd", d_scores, key_block, preferred_element_type=jnp.float32
        ) * HD ** (-0.5)
        d_keys = jnp.einsum(
            "nhqk,nqhd->nkhd", d_scores, query_block, preferred_element_type=jnp.float32
        ) * HD ** (-0.5)
        d_values = jnp.einsum(
            "nhqk,nqhd->nkhd", probs_bf, grad_block, preferred_element_type=jnp.float32
        )
        slot_part = d_keys.shape[0]
        d_kv = jnp.concatenate(
            [
                d_keys.reshape(slot_part, win_cells, INNER),
                d_values.reshape(slot_part, win_cells, INNER),
            ],
            axis=-1,
        )
        return (
            d_queries.reshape(slot_part, TILE * TILE, INNER),
            d_kv,
            jnp.sum(d_scores, axis=0, dtype=jnp.float32),
        )

    d_queries, d_kv_windows, bias_parts = lax.map(
        block_backward, (queries, key_rows, values, allowed, grad_heads)
    )
    grad_bias_sum = jnp.sum(bias_parts, axis=0)
    cell_index = jnp.arange(win_cells, dtype=jnp.int32)
    targets = (
        (start_rows[:, None] + cell_index[None, :] // win_side) * padded
        + start_cols[:, None]
        + cell_index[None, :] % win_side
    )
    grad_padded = (
        jnp.zeros((padded * padded, 2 * INNER), jnp.float32)
        .at[targets.reshape(-1)]
        .add(d_kv_windows.reshape(CAP * win_cells, 2 * INNER))
        .reshape(padded, padded, 2 * INNER)
    )
    returned = padded_2(grad_padded.astype(jnp.bfloat16), (("gy", 0), ("gx", 1)), HALO).astype(
        grad_padded.dtype
    )
    start_in = 2 * HALO
    start_far = padded + HALO
    own_grad = grad_padded[HALO : HALO + SIDE, HALO : HALO + SIDE]
    own_grad = own_grad.at[:HALO, :].add(returned[:HALO, start_in : start_in + SIDE])
    own_grad = own_grad.at[SIDE - HALO :, :].add(returned[start_far:, start_in : start_in + SIDE])
    own_grad = own_grad.at[:, :HALO].add(returned[start_in : start_in + SIDE, :HALO])
    own_grad = own_grad.at[:, SIDE - HALO :].add(returned[start_in : start_in + SIDE, start_far:])
    own_grad = own_grad.at[:HALO, :HALO].add(returned[:HALO, :HALO])
    own_grad = own_grad.at[:HALO, SIDE - HALO :].add(returned[:HALO, start_far:])
    own_grad = own_grad.at[SIDE - HALO :, :HALO].add(returned[start_far:, :HALO])
    own_grad = own_grad.at[SIDE - HALO :, SIDE - HALO :].add(returned[start_far:, start_far:])
    grad_tiles = (
        own_grad.reshape(REG, TILE, REG, TILE, 2 * INNER)
        .transpose(0, 2, 1, 3, 4)
        .reshape(REG * REG, TILE * TILE, 2 * INNER)
    )
    grad_slots = jnp.where(is_active[:, None, None], grad_tiles[tile_index], 0.0)
    grad_qkv_rows = jnp.concatenate(
        [d_queries.reshape(ROWS, INNER), grad_slots.reshape(ROWS, 2 * INNER)], axis=-1
    ).astype(jnp.bfloat16)
    grad_qkv_local = lax.dot_general(
        normed, grad_qkv_rows, (((0,), (0,)), ((), ())), preferred_element_type=jnp.float32
    )
    grad_normed = lax.dot_general(
        grad_qkv_rows, w_qkv_all, (((1,), (1,)), ((), ())), preferred_element_type=jnp.float32
    )
    scaled_grad = grad_normed * norm_gain
    gain_local = jnp.sum(grad_normed * features * inv_rms, axis=0)
    grad_tokens = (
        inv_rms * scaled_grad
        - features * inv_rms**3 * jnp.mean(scaled_grad * features, axis=-1, keepdims=True)
    ).astype(jnp.bfloat16)
    bias_local = jnp.einsum("hqk,oqk->ho", grad_bias_sum, onehot, precision=lax.Precision.HIGHEST)
    grad_gain, grad_bias = lax.psum((gain_local, bias_local), ("gy", "gx", "dp"))
    qkv_whole, out_whole = (
        lax.psum(grad_qkv_local.astype(jnp.bfloat16), ("gy", "gx")).astype(jnp.float32),
        lax.psum(grad_out_local.astype(jnp.bfloat16), ("gy", "gx")).astype(jnp.float32),
    )
    grad_qkv, grad_out = (
        lax.psum_scatter(
            qkv_whole.astype(jnp.bfloat16), "dp", scatter_dimension=0, tiled=True
        ).astype(jnp.float32),
        lax.psum_scatter(
            out_whole.astype(jnp.bfloat16), "dp", scatter_dimension=0, tiled=True
        ).astype(jnp.float32),
    )
    return (
        update.reshape(tokens.shape),
        grad_tokens.reshape(tokens.shape),
        grad_qkv,
        grad_out,
        grad_gain,
        grad_bias,
    )


def solution(mesh):
    return jax.shard_map(
        shards,
        mesh=mesh,
        in_specs=(
            P("dp", "gy", "gx", None, None),
            P("dp", None, None, None),
            P("dp", None),
            P("dp", None),
            P(),
            P(),
            P("dp", "gy", "gx", None, None),
        ),
        out_specs=(
            P("dp", "gy", "gx", None, None),
            P("dp", "gy", "gx", None, None),
            P("dp", None),
            P("dp", None),
            P(),
            P(),
        ),
        check_vma=False,
    )
```

profile of v0, /device:TPU:1, one launch (start us, length us, event | category | flops | bytes accessed | tf_op | source)
XLA Modules:
  0.0 688.7 jit_solution(10179969984633198570)
XLA Ops:
  7.2 1.0 fusion.29
  8.8 0.9 dynamic-slice_reduce_fusion
  9.7 40.1 %all_gather.6 = bf16[512,768]{1,0:T(8,128)(2,1)S(1)} all-gather(bf16[16,768]{1,0:T(8,128)(2,1)} %param.25), channel_id=1, replica_groups=mesh['gy'=4,'gx'=4,'dp'=32] {'dp'}, dimensions={0}, use_global_device_ids=true | all-gather | bytes 811008 | tf_op jit(solution)/shard_map/all_gather | solution.py:72
  49.8 1.3 convolution_convert_fusion.2
  52.2 22.8 %collective-permute-start = (bf16[3,32,512]{2,1,0:T(8,128)(2,1)S(1)}, bf16[3,32,512]{2,1,0:T(8,128)(2,1)S(1)}, u32[]{:S(2)}, u32[]{:S(2)}) collective-permute-start(bf16[3,32,512]{2,1,0:T(8,128)(2,1)S(1)} %get-tuple-element.240), channel_id=1, source_target_pairs={{0,128},{128,256},{256,384},{1,129},{129,257},{257,385},{2,130},{1... | collective-permute-start | bytes 294920 | tf_op jit(solution)/shard_map/ppermute | solution.py:26
  75.0 1.9 collective-permute-start.1
  79.4 0.7 scatter_custom_fusion.1
  80.6 4.2 while.21
  81.2 1.4 dynamic-slice.90
  83.3 1.4 dynamic-slice.90
  84.9 35.8 %all_gather.7 = bf16[256,512]{1,0:T(8,128)(2,1)S(1)} all-gather(bf16[8,512]{1,0:T(8,128)(2,1)S(1)} %copy-done.20), channel_id=1, replica_groups=mesh['gy'=4,'gx'=4,'dp'=32] {'dp'}, dimensions={0}, use_global_device_ids=true | all-gather | bytes 270336 | tf_op jit(solution)/shard_map/all_gather | solution.py:73
  120.8 0.7 broadcast_and_fusion
  121.4 1.4 fusion.16
  123.3 2.8 collective-permute-start.2
  126.1 1.5 collective-permute-start.3
  127.8 0.8 squeeze.42
  129.0 0.7 and_reduce_fusion
  129.7 0.7 copy-done.12
  130.4 1.8 collective-permute-done.3
  132.1 1.9 pad_maximum_fusion
  134.0 5.5 while.20
  134.7 2.1 bitcast_dynamic-update-slice_fusion.4
  137.4 2.1 bitcast_dynamic-update-slice_fusion.4
  139.5 1.5 copy.67
  142.3 0.8 convolution_bitcast_fusion
  144.1 0.8 fusion.23
  145.1 0.7 reshape.1052
  146.3 1.2 convert_reduce_fusion
  148.6 1.2 copy.85
  149.9 4.2 scatter_custom_fusion.2
  154.0 2.0 reshape.1056
  156.0 2.1 convert_element_type.82
  158.1 21.3 %collective-permute-start.4 = (bf16[3,38,512]{2,1,0:T(8,128)(2,1)S(1)}, bf16[3,38,512]{2,1,0:T(8,128)(2,1)S(1)}, u32[]{:S(2)}, u32[]{:S(2)}) collective-permute-start(bf16[3,38,512]{2,1,0:T(8,128)(2,1)S(1)} %get-tuple-element.236), channel_id=1, source_target_pairs={{0,128},{128,256},{256,384},{1,129},{129,257},{257,385},{2,130},{1... | collective-permute-start | bytes 350216 | tf_op jit(solution)/shard_map/ppermute | solution.py:26
  179.5 1.9 collective-permute-start.5
  181.5 1.0 convolution_convert_fusion.1
  182.4 3.5 slice.355
  186.0 3.7 collective-permute-done.5
  189.7 0.8 pad_maximum_fusion.5
  190.5 4.3 collective-permute-start.6
  194.9 1.5 collective-permute-start.7
  197.6 4.5 collective-permute-done.7
  202.0 1.7 fusion.42
  203.7 1.7 fusion.41
  205.4 1.2 convert_add_fusion.1
  206.6 3.8 scatter-add.39
  210.3 1.2 convert_add_fusion
  211.6 3.2 scatter-add.40
  214.7 0.8 convert_add_fusion.5
  215.6 1.5 scatter-add.41
  217.1 2.7 add_select_fusion
  219.8 2.8 scatter-add.44
  222.5 0.8 convert_add_fusion.4
  223.4 1.5 scatter-add.54
  224.9 0.8 slice_add_fusion
  225.7 1.5 scatter-add.55
  227.2 1.8 copy.86
  229.7 1.3 convolution_convert_fusion
  231.1 0.9 fusion.24
  232.0 2.1 fusion.25
  234.6 96.2 %all-reduce.1 = (f32[512]{0:T(512)}, f32[8,49]{1,0:T(8,128)}) all-reduce(f32[512]{0:T(512)S(1)} %get-tuple-element.204, f32[8,49]{1,0:T(8,128)S(1)} %fusion.25), channel_id=1, replica_groups=mesh['gy'=4,'gx'=4,'dp'=32] {'gy','gx','dp'}, use_global_device_ids=true, to_apply=%region_14.15 | all-reduce | flops 904 | bytes 7232 | tf_op jit(solution)/shard_map/psum | solution.py:248
  330.8 0.8 fusion.43
  331.6 66.2 %reduce-scatter.5.cloned.1.call-done = bf16[8,512]{1,0:T(8,128)(2,1)} async-done(((bf16[256,512]{1,0:T(8,128)(2,1)}), bf16[8,512]{1,0:T(8,128)(2,1)}) %reduce-scatter.5.cloned.1.call-update) | async-done | bytes 8208 | tf_op jit(solution)/shard_map/reduce_scatter | solution.py:257
  397.8 223.0 %reduce-scatter.3.cloned.1.call-done = bf16[16,768]{1,0:T(8,128)(2,1)} async-done(((bf16[512,768]{1,0:T(8,128)(2,1)}), bf16[16,768]{1,0:T(8,128)(2,1)}) %reduce-scatter.3.cloned.1.call-update) | async-done | bytes 24592 | tf_op jit(solution)/shard_map/reduce_scatter | solution.py:254
  620.8 59.8 %all-reduce.2 = (bf16[16,768]{1,0:T(8,128)(2,1)S(1)}, bf16[8,512]{1,0:T(8,128)(2,1)S(1)}) all-reduce(bf16[16,768]{1,0:T(8,128)(2,1)} %reduce-scatter.3.cloned.1.call-done, bf16[8,512]{1,0:T(8,128)(2,1)} %reduce-scatter.5.cloned.1.call-done), channel_id=1, replica_groups=mesh['gy'=4,'gx'=4,'dp'=32] {'gy','gx'}, use_global_device_ids=true, to_apply=%region_9.10 | all-reduce | flops 16384 | bytes 65536 | tf_op jit(solution)/shard_map/psum | solution.py:250
  (154 shorter events, 16.0 us)
Async XLA Ops:
  7.2 114.3 %copy-start = (f32[8,49]{1,0:T(8,128)S(1)}, f32[8,49]{1,0:T(8,128)}, u32[]{:S(2)}) copy-start(f32[8,49]{1,0:T(8,128)} %param.28) | copy-start | bytes 4708
  7.2 390.6 %reduce-scatter.5.cloned.1.call-start = ((), (), s32[]{:S(2)}) async-start(), calls=%async_computation.3 | async-start | bytes 270336 | tf_op jit(solution)/shard_map/reduce_scatter | solution.py:257
  49.8 1.4 copy-start.1
  51.9 25.6 %copy-start.21 = (s32[1,4,4,2]{2,3,1,0:T(2,128)S(1)}, s32[1,4,4,2]{2,3,1,0:T(2,128)}, u32[]{:S(2)}) copy-start(s32[1,4,4,2]{2,3,1,0:T(2,128)} %param.24) | copy-start | bytes 388
  51.9 33.0 %copy-start.20 = (bf16[8,512]{1,0:T(8,128)(2,1)S(1)}, bf16[8,512]{1,0:T(8,128)(2,1)}, u32[]{:S(2)}) copy-start(bf16[8,512]{1,0:T(8,128)(2,1)} %param.26) | copy-start | bytes 24580
  52.0 70.9 %copy-start.15 = (bf16[1,1,1,128,512]{4,3,2,1,0:T(8,128)(2,1)S(1)}, bf16[1,1,1,128,512]{4,3,2,1,0:T(8,128)(2,1)}, u32[]{:S(2)}) copy-start(bf16[1,1,1,128,512]{4,3,2,1,0:T(8,128)(2,1)} %param.29) | copy-start | bytes 393220
  52.2 71.0 %collective-permute-start = (bf16[3,32,512]{2,1,0:T(8,128)(2,1)S(1)}, bf16[3,32,512]{2,1,0:T(8,128)(2,1)S(1)}, u32[]{:S(2)}, u32[]{:S(2)}) collective-permute-start(bf16[3,32,512]{2,1,0:T(8,128)(2,1)S(1)} %get-tuple-element.240), channel_id=1, source_target_pairs={{0,128},{128,256},{256,384},{1,129},{129,257},{257,385},{2,130},{1... | collective-permute-start | bytes 294920 | tf_op jit(solution)/shard_map/ppermute | solution.py:26
  75.0 48.2 %collective-permute-start.1 = (bf16[3,32,512]{2,1,0:T(8,128)(2,1)S(1)}, bf16[3,32,512]{2,1,0:T(8,128)(2,1)S(1)}, u32[]{:S(2)}, u32[]{:S(2)}) collective-permute-start(bf16[3,32,512]{2,1,0:T(8,128)(2,1)S(1)} %get-tuple-element.241), channel_id=1, source_target_pairs={{128,0},{256,128},{384,256},{129,1},{257,129},{385,257},{130,2},{2... | collective-permute-start | bytes 294920 | tf_op jit(solution)/shard_map/ppermute | solution.py:27
  77.8 45.5 %copy-start.17 = (s32[64,196]{1,0:T(8,128)}, s32[64,196]{1,0:T(8,128)S(1)}, u32[]{:S(2)}) copy-start(s32[64,196]{1,0:T(8,128)S(1)} %fusion.57) | copy-start | bytes 150532
  78.6 44.6 %copy-start.22 = (pred[128]{0:T(512)(128)(4,1)}, pred[128]{0:T(512)(128)(4,1)S(1)}, u32[]{:S(2)}) copy-start(pred[128]{0:T(512)(128)(4,1)S(1)} %broadcast_in_dim.152) | copy-start | bytes 388
  120.7 2.2 copy-start.8
  122.9 6.1 copy-start.25
  123.3 6.4 collective-permute-start.2
  126.1 6.1 collective-permute-start.3
  129.0 15.1 %copy-start.6 = (bf16[2,64,8,32]{1,0,3,2:T(2,128)(2,1)}, bf16[2,64,8,32]{1,0,3,2:T(2,128)(2,1)S(1)}, u32[]{:S(2)}) copy-start(bf16[2,64,8,32]{1,0,3,2:T(2,128)(2,1)S(1)} %squeeze.40) | copy-start | bytes 196612
  129.7 0.7 copy-start.12
  139.5 2.2 copy-start.13
  139.5 2.8 copy-start.14
  141.5 2.6 copy-start.3
  143.1 0.9 copy-start.26
  146.3 1.2 copy-start.7
  156.0 25.4 %copy-start.10 = (bf16[128,256]{0,1:T(8,128)(2,1)S(1)}, bf16[128,256]{0,1:T(8,128)(2,1)}, u32[]{:S(2)}) copy-start(bf16[128,256]{0,1:T(8,128)(2,1)} %reshape.1052) | copy-start | bytes 196612
  156.0 25.4 %copy-start.16 = (bf16[1,1,1,128,512]{4,3,2,1,0:T(8,128)(2,1)S(1)}, bf16[1,1,1,128,512]{4,3,2,1,0:T(8,128)(2,1)}, u32[]{:S(2)}) copy-start(bf16[1,1,1,128,512]{4,3,2,1,0:T(8,128)(2,1)} %param.29) | copy-start | bytes 393220
  156.0 25.5 %copy-start.23 = (pred[128]{0:T(512)(128)(4,1)S(1)}, pred[128]{0:T(512)(128)(4,1)}, u32[]{:S(2)}) copy-start(pred[128]{0:T(512)(128)(4,1)} %copy-done.22) | copy-start | bytes 388
  158.1 27.8 %collective-permute-start.4 = (bf16[3,38,512]{2,1,0:T(8,128)(2,1)S(1)}, bf16[3,38,512]{2,1,0:T(8,128)(2,1)S(1)}, u32[]{:S(2)}, u32[]{:S(2)}) collective-permute-start(bf16[3,38,512]{2,1,0:T(8,128)(2,1)S(1)} %get-tuple-element.236), channel_id=1, source_target_pairs={{0,128},{128,256},{256,384},{1,129},{129,257},{257,385},{2,130},{1... | collective-permute-start | bytes 350216 | tf_op jit(solution)/shard_map/ppermute | solution.py:26
  179.5 10.2 %collective-permute-start.5 = (bf16[3,38,512]{2,1,0:T(8,128)(2,1)S(1)}, bf16[3,38,512]{2,1,0:T(8,128)(2,1)S(1)}, u32[]{:S(2)}, u32[]{:S(2)}) collective-permute-start(bf16[3,38,512]{2,1,0:T(8,128)(2,1)S(1)} %get-tuple-element.237), channel_id=1, source_target_pairs={{128,0},{256,128},{384,256},{129,1},{257,129},{385,257},{130,2},{2... | collective-permute-start | bytes 350216 | tf_op jit(solution)/shard_map/ppermute | solution.py:27
  185.9 10.5 %copy-start.4 = (bf16[2,196,256]{1,2,0:T(8,128)(2,1)S(1)}, bf16[2,196,256]{1,2,0:T(8,128)(2,1)}, u32[]{:S(2)}) copy-start(bf16[2,196,256]{1,2,0:T(8,128)(2,1)} %copy-done.3) | copy-start | bytes 602116
  185.9 434.9 %reduce-scatter.3.cloned.1.call-start = ((), (), s32[]{:S(2)}) async-start(), calls=%async_computation.2 | async-start | bytes 811008 | tf_op jit(solution)/shard_map/reduce_scatter | solution.py:254
  190.5 7.0 %collective-permute-start.6 = (bf16[44,3,512]{2,1,0:T(4,128)(2,1)}, bf16[44,3,512]{2,1,0:T(4,128)(2,1)S(1)}, u32[]{:S(2)}, u32[]{:S(2)}) collective-permute-start(bf16[44,3,512]{2,1,0:T(4,128)(2,1)} %get-tuple-element.234), channel_id=1, source_target_pairs={{0,32},{32,64},{64,96},{1,33},{33,65},{65,97},{2,34},{34,66},{66,9... | collective-permute-start | bytes 405512 | tf_op jit(solution)/shard_map/ppermute | solution.py:26
  194.9 7.2 %collective-permute-start.7 = (bf16[44,3,512]{2,1,0:T(4,128)(2,1)S(1)}, bf16[44,3,512]{2,1,0:T(4,128)(2,1)S(1)}, u32[]{:S(2)}, u32[]{:S(2)}) collective-permute-start(bf16[44,3,512]{2,1,0:T(4,128)(2,1)S(1)} %get-tuple-element.235), channel_id=1, source_target_pairs={{32,0},{64,32},{96,64},{33,1},{65,33},{97,65},{34,2},{66,34},{98,6... | collective-permute-start | bytes 405512 | tf_op jit(solution)/shard_map/ppermute | solution.py:27
  225.7 4.0 copy-start.5
  225.7 4.0 copy-start.19
  227.2 3.9 copy-start.9
  229.0 3.0 copy-start.11
  229.0 3.0 copy-start.18
  229.7 4.4 copy-start.2
  231.1 99.7 %copy-start.24 = (f32[128]{0:T(128)S(1)}, f32[128]{0:T(128)}, u32[]{:S(2)}) copy-start(f32[128]{0:T(128)} %get-tuple-element.244) | copy-start | bytes 1540
Sparse Core Ops, SparseCore 0:
  186.1 211.6 reduce-scatter.4
  402.8 217.9 reduce-scatter.2
where the time goes:
time: 690 us; the launch traced here: 689 us
  waiting for transfers between devices  300 us (43%)
  blocking collectives  232 us (34%)
  starting transfers between devices  58.1 us (8%)
  local copies, waits for them, and re-layouts  44.6 us (6%)
  other arithmetic  27.4 us (4%)
  between operations  14.9 us (2%)
  matrix products  12.1 us (2%)
    reduce_scatter x1, waiting for transfers between devices, shards(): lax.psum_scatter(qkv_whole.astype(jnp.bfloat16), 'dp', scatter_dimension=...  223 us
    psum x1, blocking collectives, shards(): lax.psum((gain_local, bias_local), ('gy', 'gx', 'dp'))  96.2 us
    reduce_scatter x1, waiting for transfers between devices, shards(): lax.psum_scatter(out_whole.astype(jnp.bfloat16), 'dp', scatter_dimension=...  66.2 us
    psum x1, blocking collectives, shards(): lax.psum(grad_qkv_local.astype(jnp.bfloat16), ('gy', 'gx'))  59.8 us
    ppermute x4, starting transfers between devices, padded_2(): before = lax.ppermute(last, axis, up)  51.2 us
    all_gather x1, blocking collectives, shards(): lax.all_gather(w_qkv, 'dp', axis=0, tiled=True)  40.1 us
    all_gather x1, blocking collectives, shards(): lax.all_gather(w_out, 'dp', axis=0, tiled=True)  35.8 us
  transfers between devices with their start and end apart: 10, of which 6 were waited for; matrix products, arithmetic and copies ran while one was open for 7% of the time, Pallas kernels for 0%

commit v1 on v0

v1 whole, which is shorter than its diff:
```python
import functools

import jax
import jax.numpy as jnp
from jax import lax
from jax.experimental import pallas as pl
from jax.experimental.pallas import tpu as pltpu
from jax.sharding import PartitionSpec as P

D = 512
HEADS = 8
HD = 32
INNER = 256
TILE = 8
HALO = 3
REG = 4
CAP = 2
ROWS = 128
CELLS = TILE * TILE
DP = 32
NX = 4
NY = 8
REGIONS = 9
OWN = 4
TILES = REGIONS * CAP
BROWS = HEADS * CELLS
CHUNK = 128
CHUNKS = BROWS // CHUNK
FAR = 9
SCALE = HD ** (-0.5)
WROWS = 64
SMALL = 16
CORES = [[0, 1], [2, 3]]
XS = [[x * NY + y for x in range(NX)] for y in range(NY)]
YS = [[x * NY + y for y in range(NY)] for x in range(NX)]
F32 = jnp.float32
BF = jnp.bfloat16
NT = (((1,), (1,)), ((), ()))
TN = (((0,), (0,)), ((), ()))
VM = pl.BlockSpec(memory_space=pltpu.VMEM)
SM = pl.BlockSpec(memory_space=pltpu.SMEM)


def dot(a, b, dims=(((1,), (0,)), ((), ()))):
    return lax.dot_general(a, b, dims, preferred_element_type=F32)


def call(body, outs, ins, scratch=(), limit=16, flops=1000000, traffic=1000000):
    single = not isinstance(outs, (list, tuple))
    return pl.pallas_call(
        body,
        out_shape=outs,
        in_specs=ins,
        out_specs=VM if single else [VM] * len(outs),
        scratch_shapes=list(scratch),
        compiler_params=pltpu.CompilerParams(vmem_limit_bytes=limit * 2**20),
        cost_estimate=pl.CostEstimate(flops=flops, bytes_accessed=traffic, transcendentals=0),
    )


def shape(dims, dtype):
    return jax.ShapeDtypeStruct(dims, dtype)


def pack_body(place, wq, wo, tok, grad, w_out, x_out):
    core = place[2]

    def half(c):
        rows = [wq[:, (3 * c + j) * 128 : (3 * c + j + 1) * 128].astype(F32) for j in range(3)]
        rows += [wo[:, (2 * c + j) * 128 : (2 * c + j + 1) * 128].astype(F32) for j in range(2)]
        block = jnp.concatenate(rows, axis=0).astype(BF)
        for d in range(DP):
            w_out[d] = block

    pl.when(core == 0)(lambda: half(0))
    pl.when(core == 1)(lambda: half(1))
    x_out[:, 0:D] = tok[...]
    x_out[:, D : 2 * D] = grad[...]


def table_body(base_ref, tab):
    query = lax.broadcasted_iota(jnp.int32, (CELLS, 128), 0)
    lane = lax.broadcasted_iota(jnp.int32, (CELLS, 128), 1)
    key = lane & 63
    left = lane < 64
    row_step = (key >> 3) - (query >> 3)
    col_step = (key & 7) - (query & 7)
    base = base_ref[...]
    for place in range(9):
        down, across = place // 3 - 1, place % 3 - 1
        shift = 64 * down + 8 * across
        inside = (jnp.abs(row_step + 8 * down) <= HALO) & (jnp.abs(col_step + 8 * across) <= HALO)
        first = pltpu.roll(base, (-shift - 27) % 128, 1)
        second = pltpu.roll(base, (64 - shift - 27) % 128, 1)
        for h in range(HEADS):
            a = pltpu.roll(
                jnp.broadcast_to(first[h : h + 1], (CELLS, 128)), 0, 1, stride=1, stride_axis=0
            )
            b = pltpu.roll(
                jnp.broadcast_to(second[h : h + 1], (CELLS, 128)), 0, 1, stride=1, stride_axis=0
            )
            tab[place, h * CELLS : (h + 1) * CELLS, :] = jnp.where(
                inside, jnp.where(left, a, b), -jnp.inf
            )
    tab[FAR] = jnp.full((BROWS, 128), -jnp.inf, F32)


def main_body(
    place,
    tiles,
    left,
    mid,
    right,
    w_mine,
    w_other,
    gain,
    tab,
    update,
    grad_tokens,
    sums,
    crow,
    ccol,
    blocks,
    wq,
    wo,
    normed,
    qkv,
    gatt,
    qbd,
    gbd,
    scores,
    dprobs,
    top,
    total,
    delta,
    pbf,
    dsf,
    att,
    dq,
    attended,
    dqkv,
    dk,
    dv,
    hist,
    rowsum,
):
    my_row, my_col, core = place[0], place[1], place[2]

    def assemble(pair):
        for c, w in enumerate(pair):
            for j in range(3):
                wq[:, (3 * c + j) * 128 : (3 * c + j + 1) * 128] = w[
                    :, 16 * j : 16 * j + 16, :
                ].reshape(D, 128)
            both = w[:, 48:64, :].astype(F32)
            for j in range(2):
                wo[:, (2 * c + j) * 128 : (2 * c + j + 1) * 128] = (
                    both[:, 8 * j : 8 * j + 8, :].reshape(INNER, 128).astype(BF)
                )

    pl.when(core == 0)(lambda: assemble((w_mine, w_other)))
    pl.when(core == 1)(lambda: assemble((w_other, w_mine)))

    for t in range(TILES):
        r = t // CAP
        ry, rx = my_row + r // 3 - 1, my_col + r % 3 - 1
        there = (ry >= 0) & (ry < 4) & (rx >= 0) & (rx < 4)
        tile = tiles[jnp.clip(ry, 0, 3), jnp.clip(rx, 0, 3), t % CAP]
        crow[t] = jnp.where(there, ry * REG + (tile >> 2), -1000 * (t + 1))
        ccol[t] = jnp.where(there, rx * REG + (tile & 3), -1000 * (t + 1))

    gain_row = gain[...]
    for r in range(REGIONS):
        source = (left, mid, right)[r % 3]
        x = source[r // 3, :, 0:D].astype(F32)
        inv = lax.rsqrt(jnp.mean(x * x, axis=-1, keepdims=True) + 1e-06)
        n = (x * inv * gain_row).astype(BF)
        normed[r * ROWS : (r + 1) * ROWS, :] = n
        qkv[r * ROWS : (r + 1) * ROWS, :] = dot(n, wq[...]).astype(BF)
        gatt[r * ROWS : (r + 1) * ROWS, :] = dot(
            source[r // 3, :, D : 2 * D], wo[...], NT
        ).astype(BF)

    dk[...] = jnp.zeros_like(dk)
    dv[...] = jnp.zeros_like(dv)
    hist[...] = jnp.zeros_like(hist)
    head_of = lax.broadcasted_iota(jnp.int32, (1, INNER), 1) >> 5
    masks = [(head_of == h).astype(F32) for h in range(HEADS)]
    masks_bf = [m.astype(BF) for m in masks]
    lane = lax.broadcasted_iota(jnp.int32, (CHUNK, 128), 1)
    first_slot = lane < 64
    flip = ((lane ^ lax.broadcasted_iota(jnp.int32, (CHUNK, 128), 0)) == 63).astype(F32).astype(BF)

    def near(a, b):
        return (jnp.abs(crow[a] - crow[b]) <= 1) & (jnp.abs(ccol[a] - ccol[b]) <= 1)

    def offset(a, b):
        index = (crow[b] - crow[a] + 1) * 3 + ccol[b] - ccol[a] + 1
        return jnp.where(near(a, b), index, FAR)

    def process(i, own):
        at = pl.multiple_of(i * CELLS, CELLS)
        queries = qkv[pl.ds(at, CELLS), 0:INNER]
        grads = gatt[pl.ds(at, CELLS), :]
        for h in range(HEADS):
            qbd[h * CELLS : (h + 1) * CELLS, :] = queries * masks_bf[h]
            gbd[h * CELLS : (h + 1) * CELLS, :] = grads * masks_bf[h]
        count = jnp.int32(0)
        own_block = jnp.int32(0)
        for r in range(REGIONS):
            blocks[count] = r
            if r == OWN:
                own_block = count
            count = count + (near(i, 2 * r) | near(i, 2 * r + 1)).astype(jnp.int32)
        top[...] = jnp.full(top.shape, -jnp.inf, F32)
        total[...] = jnp.zeros_like(total)
        delta[...] = jnp.zeros_like(delta)

        def pass_a(b, carry):
            r = blocks[b]
            k_at = pl.multiple_of(r * ROWS, ROWS)
            keys = qkv[pl.ds(k_at, ROWS), INNER : 2 * INNER]
            values = qkv[pl.ds(k_at, ROWS), 2 * INNER : 3 * INNER]
            off_a, off_b = offset(i, 2 * r), offset(i, 2 * r + 1)
            for c in range(CHUNKS):
                rows = slice(c * CHUNK, (c + 1) * CHUNK)
                bias = jnp.where(first_slot, tab[off_a, rows, :], tab[off_b, rows, :])
                s = dot(qbd[rows, :], keys, NT) * SCALE + bias
                scores[b, rows, :] = s
                top[rows, :] = jnp.maximum(top[rows, :], s)
                dprobs[b, rows, :] = dot(gbd[rows, :], values, NT)
            return carry

        lax.fori_loop(0, count, pass_a, 0)
        for c in range(CHUNKS):
            rows = slice(c * CHUNK, (c + 1) * CHUNK)
            top[rows, :] = jnp.broadcast_to(
                jnp.max(top[rows, :], axis=-1, keepdims=True), (CHUNK, 128)
            )

        def pass_b(b, carry):
            for c in range(CHUNKS):
                rows = slice(c * CHUNK, (c + 1) * CHUNK)
                e = jnp.exp(scores[b, rows, :] - top[rows, :])
                scores[b, rows, :] = e
                total[rows, :] += e
                delta[rows, :] += e * dprobs[b, rows, :]
            return carry

        lax.fori_loop(0, count, pass_b, 0)
        for c in range(CHUNKS):
            rows = slice(c * CHUNK, (c + 1) * CHUNK)
            inverse = 1.0 / jnp.sum(total[rows, :], axis=-1, keepdims=True)
            d = jnp.sum(delta[rows, :], axis=-1, keepdims=True) * inverse
            total[rows, :] = jnp.broadcast_to(inverse, (CHUNK, 128))
            delta[rows, :] = jnp.broadcast_to(d, (CHUNK, 128))
        if own:
            att[...] = jnp.zeros_like(att)
            dq[...] = jnp.zeros_like(dq)

        def probs_of(b):
            for c in range(CHUNKS):
                rows = slice(c * CHUNK, (c + 1) * CHUNK)
                p = scores[b, rows, :] * total[rows, :]
                pbf[rows, :] = p.astype(BF)
                dsf[rows, :] = (p * (dprobs[b, rows, :] - delta[rows, :])).astype(BF)

        def to_keys():
            dk[...] += dot(dsf[...], qbd[...], TN)
            dv[...] += dot(pbf[...], gbd[...], TN)

        def pass_c(b, carry):
            r = blocks[b]
            k_at = pl.multiple_of(r * ROWS, ROWS)
            keys = qkv[pl.ds(k_at, ROWS), INNER : 2 * INNER]
            values = qkv[pl.ds(k_at, ROWS), 2 * INNER : 3 * INNER]
            probs_of(b)
            pl.when(r == OWN)(to_keys)
            att_sum = att[...]
            dq_sum = dq[...]
            for h in range(HEADS):
                rows = slice(h * CELLS, (h + 1) * CELLS)
                att_sum += dot(pbf[rows, :], values) * masks[h]
                dq_sum += dot(dsf[rows, :], keys) * masks[h]
            att[...] = att_sum
            dq[...] = dq_sum
            half = first_slot[0:CELLS]
            for c in range(CHUNKS):
                flipped = dot(flip, dsf[c * CHUNK : (c + 1) * CHUNK, :])
                for h in range(2):
                    ds = flipped[h * CELLS : (h + 1) * CELLS, :]
                    for s, part in enumerate((jnp.where(half, ds, 0.0), jnp.where(half, 0.0, ds))):
                        turned = pltpu.roll(part, 0, 1, stride=1, stride_axis=0)
                        rowsum[s, 2 * c + h : 2 * c + h + 1, :] = jnp.sum(
                            turned, axis=0, keepdims=True
                        )
            for s in range(CAP):
                t = 2 * r + s
                shift = 64 * (crow[t] - crow[i]) + 8 * (ccol[t] - ccol[i]) - 36 - 64 * s
                shift = jnp.where(near(i, t), shift, 0) + 256
                hist[...] += pltpu.roll(rowsum[s], shift & 127, 1)
            return carry

        if own:
            lax.fori_loop(0, count, pass_c, 0)
            slot_at = pl.multiple_of((i - OWN * CAP) * CELLS, CELLS)
            attended[pl.ds(slot_at, CELLS), :] = att[...].astype(BF)
            dqkv[pl.ds(slot_at, CELLS), 0:INNER] = (dq[...] * SCALE).astype(BF)
        else:
            probs_of(own_block)
            to_keys()

    def own_step(s, carry):
        process(OWN * CAP + s, True)
        return carry

    lax.fori_loop(0, CAP, own_step, 0)

    def other_step(i, carry):
        t = i + jnp.where(i >= OWN * CAP, CAP, 0)
        pl.when(near(t, OWN * CAP) | near(t, OWN * CAP + 1))(lambda: process(t, False))
        return carry

    lax.fori_loop(0, TILES - CAP, other_step, 0)

    dqkv[:, INNER : 2 * INNER] = (dk[...] * SCALE).astype(BF)
    dqkv[:, 2 * INNER : 3 * INNER] = dv[...].astype(BF)
    update[...] = dot(attended[...], wo[...]).astype(BF)
    grad_out = dot(attended[...], mid[1, :, D : 2 * D], TN)
    for c in range(2):
        pair = [
            grad_out[:, (2 * c + j) * 128 : (2 * c + j + 1) * 128].reshape(DP, 8, 128)
            for j in range(2)
        ]
        both = jnp.concatenate(pair, axis=1).astype(BF)
        for d in range(DP):
            sums[c, d * WROWS + 48 : d * WROWS + 64, :] = both[d]
    own_rows = slice(OWN * ROWS, (OWN + 1) * ROWS)
    for j in range(6):
        block = dot(normed[own_rows, :], dqkv[:, j * 128 : (j + 1) * 128], TN).astype(BF)
        for d in range(DP):
            at = d * WROWS + (j % 3) * 16
            sums[j // 3, at : at + 16, :] = block[d * 16 : (d + 1) * 16]
    d_normed = dot(dqkv[...], wq[...], NT)
    x = mid[1, :, 0:D].astype(F32)
    inv = lax.rsqrt(jnp.mean(x * x, axis=-1, keepdims=True) + 1e-06)
    scaled = d_normed * gain_row
    gain_sum = jnp.sum(d_normed * x * inv, axis=0, keepdims=True)
    grad_tokens[...] = (
        inv * scaled - x * (inv * inv * inv) * jnp.mean(scaled * x, axis=-1, keepdims=True)
    ).astype(BF)
    folded = hist[0:4, :] + pltpu.roll(hist[4:8, :], 64, 1)
    small = jnp.concatenate([gain_sum[:, j * 128 : (j + 1) * 128] for j in range(4)] + [folded], 0)
    split = halves(small)
    sums[0, DP * WROWS : DP * WROWS + SMALL, :] = split
    sums[1, DP * WROWS : DP * WROWS + SMALL, :] = split


def halves(value):
    high = value.astype(BF).astype(F32)
    return jnp.concatenate([high, value - high], axis=0).astype(BF)


def whole(value):
    wide = value.astype(F32)
    return wide[..., 0:8, :] + wide[..., 8:16, :]


def sum_body(senders, parts, span, received, out):
    rows = parts * span
    for p in range(parts):
        acc = received[0, p * span : (p + 1) * span, :].astype(F32)
        for s in range(1, senders):
            acc += received[s, p * span : (p + 1) * span, :].astype(F32)
        out[p, 0:span, :] = acc.astype(BF)
    small = whole(received[0, rows : rows + SMALL, :])
    for s in range(1, senders):
        small += whole(received[s, rows : rows + SMALL, :])
    split = halves(small)
    for p in range(parts):
        out[p, span : span + SMALL, :] = split


def last_sum_body(received, out):
    acc = received[0, 0:WROWS, :].astype(F32)
    small = whole(received[0, WROWS : WROWS + SMALL, :])
    for s in range(1, NY):
        acc += received[s, 0:WROWS, :].astype(F32)
        small += whole(received[s, WROWS : WROWS + SMALL, :])
    acc = acc.astype(BF)
    split = halves(small)
    for p in range(16):
        out[p, 0:WROWS, :] = acc
        out[p, WROWS : WROWS + SMALL, :] = split


def finish_body(received, grad_qkv, grad_out, grad_gain, grad_bias):
    small = None
    for c in range(2):
        acc = None
        for y in range(c, 4, 2):
            for x in range(4):
                part = received[4 * y + x, 0:WROWS, :].astype(F32)
                acc = part if acc is None else acc + part
                if c == 0:
                    more = whole(received[4 * y + x, WROWS : WROWS + SMALL, :])
                    small = more if small is None else small + more
        for j in range(3):
            grad_qkv[:, (3 * c + j) * 128 : (3 * c + j + 1) * 128] = acc[16 * j : 16 * j + 16, :]
        for j in range(2):
            at = 48 + 8 * j
            grad_out[:, (2 * c + j) * 128 : (2 * c + j + 1) * 128] = acc[at : at + 8, :]
    for j in range(4):
        grad_gain[:, j * 128 : (j + 1) * 128] = small[j : j + 1, :]
    folded = small[4:8, :]
    table = jnp.concatenate([folded, pltpu.roll(folded, 64, 1)], axis=0)
    lane = lax.broadcasted_iota(jnp.int32, (HEADS, 128), 1)
    out = jnp.zeros((HEADS, 128), F32)
    for r in range(7):
        moved = table if r == 0 else pltpu.roll(table, 128 - r, 1)
        out = jnp.where((lane >= 7 * r) & (lane < 7 * r + 7), moved, out)
    grad_bias[...] = out[:, 0:49]


def shards(tokens, tile_ids, w_qkv, w_out, norm_gain, rel_bias, update_grad):
    my_row = lax.axis_index("gy")
    my_col = lax.axis_index("gx")
    place = jnp.stack([my_row, my_col, my_row % 2]).astype(jnp.int32)
    swap = [(0, 1), (1, 0), (2, 3), (3, 2)]
    forth = [(0, 1), (1, 2), (2, 3)]
    back = [(1, 0), (2, 1), (3, 2)]

    w_send, rows = call(
        pack_body,
        [shape((DP, WROWS, 128), BF), shape((ROWS, 2 * D), BF)],
        [SM, VM, VM, VM, VM],
    )(place, w_qkv, w_out, tokens.reshape(ROWS, D), update_grad.reshape(ROWS, D))
    above = lax.ppermute(rows, "gy", forth)
    below = lax.ppermute(rows, "gy", back)
    w_mine = lax.all_to_all(w_send, "dp", 0, 0, tiled=True)
    mid = jnp.stack([above, rows, below])
    left = lax.ppermute(mid, "gx", forth)
    right = lax.ppermute(mid, "gx", back)
    w_other = lax.ppermute(w_mine, "gy", swap)

    base = jnp.pad(rel_bias.reshape(HEADS, 7, 7), ((0, 0), (0, 0), (0, 1))).reshape(HEADS, 56)
    base = jnp.pad(base, ((0, 0), (0, 72)))
    table = call(table_body, shape((10, BROWS, 128), F32), [VM])(base)

    f32 = lambda *dims: pltpu.VMEM(dims, F32)
    bf = lambda *dims: pltpu.VMEM(dims, BF)
    update, grad_tokens, sums = call(
        main_body,
        [
            shape((ROWS, D), BF),
            shape((ROWS, D), BF),
            shape((2, DP * WROWS + SMALL, 128), BF),
        ],
        [SM, SM] + [VM] * 7,
        [
            pltpu.SMEM((TILES,), jnp.int32),
            pltpu.SMEM((TILES,), jnp.int32),
            pltpu.SMEM((REGIONS + 1,), jnp.int32),
            bf(D, 3 * INNER),
            bf(INNER, D),
            bf(REGIONS * ROWS, D),
            bf(REGIONS * ROWS, 3 * INNER),
            bf(REGIONS * ROWS, INNER),
            bf(BROWS, INNER),
            bf(BROWS, INNER),
            f32(4, BROWS, 128),
            f32(4, BROWS, 128),
            f32(BROWS, 128),
            f32(BROWS, 128),
            f32(BROWS, 128),
            bf(BROWS, 128),
            bf(BROWS, 128),
            f32(CELLS, INNER),
            f32(CELLS, INNER),
            bf(ROWS, INNER),
            bf(ROWS, 3 * INNER),
            f32(ROWS, INNER),
            f32(ROWS, INNER),
            f32(HEADS, 128),
            f32(CAP, HEADS, 128),
        ],
        limit=40,
        flops=4000000000,
        traffic=12000000,
    )(
        place,
        tile_ids.reshape(4, 4, CAP),
        left,
        mid,
        right,
        w_mine,
        w_other,
        norm_gain.reshape(1, D),
        table,
    )

    got = lax.all_to_all(sums, "gy", 0, 0, tiled=True, axis_index_groups=CORES)
    got = call(
        functools.partial(sum_body, 2, NX, NY * WROWS),
        shape((NX, NY * WROWS + SMALL, 128), BF),
        [VM],
    )(got)
    got = lax.all_to_all(got, "dp", 0, 0, tiled=True, axis_index_groups=XS)
    got = call(
        functools.partial(sum_body, NX, NY, WROWS), shape((NY, WROWS + SMALL, 128), BF), [VM]
    )(got)
    got = lax.all_to_all(got, "dp", 0, 0, tiled=True, axis_index_groups=YS)
    got = call(last_sum_body, shape((16, WROWS + SMALL, 128), BF), [VM])(got)
    got = lax.all_to_all(got, ("gy", "gx"), 0, 0, tiled=True)
    grad_qkv, grad_out, grad_gain, grad_bias = call(
        finish_body,
        [
            shape((16, 3 * INNER), F32),
            shape((8, D), F32),
            shape((1, D), F32),
            shape((HEADS, 49), F32),
        ],
        [VM],
    )(got)
    return (
        update.reshape(tokens.shape),
        grad_tokens.reshape(tokens.shape),
        grad_qkv,
        grad_out,
        grad_gain.reshape(D),
        grad_bias,
    )


def solution(mesh):
    return jax.shard_map(
        shards,
        mesh=mesh,
        in_specs=(
            P("dp", "gy", "gx", None, None),
            P("dp", None, None, None),
            P("dp", None),
            P("dp", None),
            P(),
            P(),
            P("dp", "gy", "gx", None, None),
        ),
        out_specs=(
            P("dp", "gy", "gx", None, None),
            P("dp", "gy", "gx", None, None),
            P("dp", None),
            P("dp", None),
            P(),
            P(),
        ),
        check_vma=False,
    )
```

time: 690 us -> 128 us (0.19)
  waiting for transfers between devices: 300 us -> 14.7 us
  blocking collectives: 232 us -> 62.5 us
  local copies, waits for them, and re-layouts: 44.6 us -> 3.53 us
  other arithmetic: 27.4 us -> 0.16 us
  starting transfers between devices: 58.1 us -> 31.3 us
  between operations: 14.9 us -> 0.75 us
  Pallas kernels: 0 us -> 14.1 us
  matrix products: 12.1 us -> 0 us
    reduce_scatter x2 -> x0, waiting for transfers between devices: 289 us -> none  [the longest x1 223 us: shards(): lax.psum_scatter(qkv_whole.astype(jnp.bfloat16), 'dp', scatter_dimension=...]
    psum x2 -> x0, blocking collectives: 156 us -> none  [the longest x1 96.2 us: shards(): lax.psum((gain_local, bias_local), ('gy', 'gx', 'dp'))]
    all_gather x2 -> x0, blocking collectives: 75.9 us -> none  [the longest x1 40.1 us: shards(): lax.all_gather(w_qkv, 'dp', axis=0, tiled=True)]
    all_to_all x0 -> x4, blocking collectives: none -> 62.5 us  [the longest x1 26.7 us: shards(): got = lax.all_to_all(got, ('gy', 'gx'), 0, 0, tiled=True)]
    ppermute x8 -> x5, starting transfers between devices: 58 us -> 20.6 us  [the longest x1 10.5 us: shards(): above = lax.ppermute(rows, 'gy', forth)]
    scatter-add x6 -> x0, local copies, waits for them, and re-layouts: 14.2 us -> none  [the longest x1 3.76 us: shards(): own_grad.at[:, :HALO].add(returned[start_in:start_in + SIDE, :HALO])]
    pallas_call x0 -> x7, Pallas kernels: none -> 14.1 us  [the longest x1 10.9 us: shards(): call(main_body, [shape((ROWS, D), BF), shape((ROWS, D), BF), shape((2, DP...]
    gather x18 -> x0, local copies, waits for them, and re-layouts: 11.7 us -> none
  transfers between devices with their start and end apart: 10 -> 6, of which waited for: 6 -> 4; matrix products, arithmetic and copies ran while one was open for 7% -> 0% of each run, Pallas kernels for 0% -> 1%
where the time goes in v1:
time: 128 us; the launch traced here: 127 us
  blocking collectives  62.5 us (49%)
  starting transfers between devices  31.3 us (24%)
  waiting for transfers between devices  14.7 us (11%)
  Pallas kernels  14.1 us (11%)
  local copies, waits for them, and re-layouts  3.53 us (3%)
    all_to_all x1, blocking collectives, shards(): got = lax.all_to_all(got, ('gy', 'gx'), 0, 0, tiled=True)  26.7 us
    all_to_all x1, blocking collectives, shards(): got = lax.all_to_all(got, 'dp', 0, 0, tiled=True, axis_index_groups=XS)  16.7 us
    all_to_all x1, blocking collectives, shards(): got = lax.all_to_all(got, 'dp', 0, 0, tiled=True, axis_index_groups=YS)  15 us
    pallas_call x1, Pallas kernels, shards(): call(main_body, [shape((ROWS, D), BF), shape((ROWS, D), BF), shape((2, DP...  10.9 us
    all_to_all x1, starting transfers between devices, shards(): w_mine = lax.all_to_all(w_send, 'dp', 0, 0, tiled=True)  10.6 us
    ppermute x1, starting transfers between devices, shards(): above = lax.ppermute(rows, 'gy', forth)  10.5 us
    ppermute x1, waiting for transfers between devices, shards(): above = lax.ppermute(rows, 'gy', forth)  6.32 us
    ppermute x1, waiting for transfers between devices, shards(): right = lax.ppermute(mid, 'gx', back)  4.44 us
  transfers between devices with their start and end apart: 6, of which 4 were waited for; matrix products, arithmetic and copies ran while one was open for 0% of the time, Pallas kernels for 1%

profile of v1, /device:TPU:1, one launch (start us, length us, event | category | flops | bytes accessed | tf_op | source)
XLA Modules:
  0.0 126.9 jit_solution(444430374320227754)
XLA Ops:
  0.6 0.1 pad_add_fusion.place
  0.7 0.0 copy-start
  0.7 0.9 copy-done
  1.6 0.0 copy-start.1
  1.6 0.9 copy-done.1
  2.5 0.0 copy-start.2
  2.5 0.7 copy-done.2
  3.3 0.0 copy-start.3
  3.3 0.7 copy-done.3
  4.0 1.5 %shard_map.118 = (bf16[32,64,128]{2,1,0:T(8,128)(2,1)}, bf16[128,1024]{1,0:T(8,128)(2,1)S(1)}) custom-call(s32[3]{0:T(128)S(1)} %pad_add_fusion.place, bf16[16,768]{1,0:T(8,128)(2,1)S(1)} %copy-done.2, bf16[8,512]{1,0:T(8,128)(2,1)S(1)} %copy-done.3, bf16[128,512]{1,0:T(8,128)(2,1)S(1)} %bitcast.14, bf16[128,512]{1,0:T(8,128)(2,1)S(1)} %bitcast.15), custom_call_target="tpu_custom_call" | custom-call | flops 1000000 | bytes 1000000 | tf_op jit(solution)/shard_map/pallas_call | solution.py:433
  5.4 0.0 copy-start.5
  5.4 10.6 %all-to-all-start = ((bf16[32,64,128]{2,1,0:T(8,128)(2,1)}), bf16[32,64,128]{2,1,0:T(8,128)(2,1)S(1)}, u32[]{:S(2)}, u32[]{:S(2)}) async-start(bf16[32,64,128]{2,1,0:T(8,128)(2,1)} %get-tuple-element.16), calls=%async_computation | async-start | bytes 1048576 | tf_op jit(solution)/shard_map/all_to_all | solution.py:440
  16.1 0.0 copy-start.6
  16.1 2.9 %collective-permute-start.1 = (bf16[128,1024]{1,0:T(8,128)(2,1)S(1)}, bf16[128,1024]{1,0:T(8,128)(2,1)S(1)}, u32[]{:S(2)}, u32[]{:S(2)}) collective-permute-start(bf16[128,1024]{1,0:T(8,128)(2,1)S(1)} %get-tuple-element.15), channel_id=1, source_target_pairs={{128,0},{256,128},{384,256},{129,1},{257,129},{385,257},{130,2},{2... | collective-permute-start | bytes 786440 | tf_op jit(solution)/shard_map/ppermute | solution.py:439
  19.0 10.5 %collective-permute-start = (bf16[128,1024]{1,0:T(8,128)(2,1)S(1)}, bf16[128,1024]{1,0:T(8,128)(2,1)S(1)}, u32[]{:S(2)}, u32[]{:S(2)}) collective-permute-start(bf16[128,1024]{1,0:T(8,128)(2,1)S(1)} %get-tuple-element.15), channel_id=1, source_target_pairs={{0,128},{128,256},{256,384},{1,129},{129,257},{257,385},{2,130},{1... | collective-permute-start | bytes 786440 | tf_op jit(solution)/shard_map/ppermute | solution.py:438
  29.5 2.4 %collective-permute-done.1 = bf16[128,1024]{1,0:T(8,128)(2,1)S(1)} collective-permute-done((bf16[128,1024]{1,0:T(8,128)(2,1)S(1)}, bf16[128,1024]{1,0:T(8,128)(2,1)S(1)}, u32[]{:S(2)}, u32[]{:S(2)}) %collective-permute-start.1) | collective-permute-done | bytes 262176 | tf_op jit(solution)/shard_map/ppermute | solution.py:439
  31.9 6.3 %collective-permute-done = bf16[128,1024]{1,0:T(8,128)(2,1)S(1)} collective-permute-done((bf16[128,1024]{1,0:T(8,128)(2,1)S(1)}, bf16[128,1024]{1,0:T(8,128)(2,1)S(1)}, u32[]{:S(2)}, u32[]{:S(2)}) %collective-permute-start) | collective-permute-done | bytes 262176 | tf_op jit(solution)/shard_map/ppermute | solution.py:438
  38.2 0.1 pad_maximum_fusion.mid
  38.3 1.3 %collective-permute-start.3 = (bf16[3,128,1024]{2,1,0:T(8,128)(2,1)S(1)}, bf16[3,128,1024]{2,1,0:T(8,128)(2,1)S(1)}, u32[]{:S(2)}, u32[]{:S(2)}) collective-permute-start(bf16[3,128,1024]{2,1,0:T(8,128)(2,1)S(1)} %pad_maximum_fusion.mid), channel_id=1, source_target_pairs={{32,0},{64,32},{96,64},{33,1},{65,33},{97,65},{34,2},{66,34},{98,6... | collective-permute-start | bytes 2359304 | tf_op jit(solution)/shard_map/ppermute | solution.py:443
  39.6 4.0 %collective-permute-start.2 = (bf16[3,128,1024]{2,1,0:T(8,128)(2,1)S(1)}, bf16[3,128,1024]{2,1,0:T(8,128)(2,1)S(1)}, u32[]{:S(2)}, u32[]{:S(2)}) collective-permute-start(bf16[3,128,1024]{2,1,0:T(8,128)(2,1)S(1)} %pad_maximum_fusion.mid), channel_id=1, source_target_pairs={{0,32},{32,64},{64,96},{1,33},{33,65},{65,97},{2,34},{34,66},{66,9... | collective-permute-start | bytes 2359304 | tf_op jit(solution)/shard_map/ppermute | solution.py:442
  43.7 0.0 all-to-all-done.w_mine
  43.7 1.9 %collective-permute-start.4 = (bf16[32,64,128]{2,1,0:T(8,128)(2,1)S(1)}, bf16[32,64,128]{2,1,0:T(8,128)(2,1)}, u32[]{:S(2)}, u32[]{:S(2)}) collective-permute-start(bf16[32,64,128]{2,1,0:T(8,128)(2,1)S(1)} %all-to-all-done.w_mine), channel_id=1, source_target_pairs={{0,128},{128,0},{256,384},{384,256},{1,129},{129,1},{257,385},{385... | collective-permute-start | bytes 1572872 | tf_op jit(solution)/shard_map/ppermute | solution.py:444
  45.6 0.0 copy-done.5
  45.6 0.1 copy.16.tiles
  45.7 0.0 copy-done.6
  45.7 0.1 reshape.43
  45.8 0.1 reshape.44
  45.9 0.0 copy-start.4
  45.9 0.7 shard_map.119.tab
  46.6 4.4 %collective-permute-done.3.right = bf16[3,128,1024]{2,1,0:T(8,128)(2,1)S(1)} collective-permute-done((bf16[3,128,1024]{2,1,0:T(8,128)(2,1)S(1)}, bf16[3,128,1024]{2,1,0:T(8,128)(2,1)S(1)}, u32[]{:S(2)}, u32[]{:S(2)}) %collective-permute-start.3) | collective-permute-done | bytes 786464 | tf_op jit(solution)/shard_map/ppermute | solution.py:443
  51.1 1.5 %collective-permute-done.2.left = bf16[3,128,1024]{2,1,0:T(8,128)(2,1)S(1)} collective-permute-done((bf16[3,128,1024]{2,1,0:T(8,128)(2,1)S(1)}, bf16[3,128,1024]{2,1,0:T(8,128)(2,1)S(1)}, u32[]{:S(2)}, u32[]{:S(2)}) %collective-permute-start.2) | collective-permute-done | bytes 786464 | tf_op jit(solution)/shard_map/ppermute | solution.py:442
  52.5 0.0 collective-permute-done.4.w_other
  52.5 0.0 copy-done.4
  52.5 10.9 %shard_map.120 = (bf16[128,512]{1,0:T(8,128)(2,1)}, bf16[128,512]{1,0:T(8,128)(2,1)}, bf16[2,2064,128]{2,1,0:T(8,128)(2,1)S(1)}) custom-call(s32[3]{0:T(128)S(1)} %pad_add_fusion.place, s32[4,4,2]{2,1,0:T(4,128)S(1)} %copy.16.tiles, bf16[3,128,1024]{2,1,0:T(8,128)(2,1)S(1)} %collective-permute-done.2.left, bf16[3,128,1024]{2,1,0:T(8,128)(2,1)S(1)} %pad_maximum_fusion.mid, ...), custom_call_target="tpu_custom_call" | custom-call | flops 4000000000 | bytes 12000000 | tf_op jit(solution)/shard_map/pallas_call | solution.py:452
  63.5 4.2 %all_to_all.25.received = bf16[2,2064,128]{2,1,0:T(8,128)(2,1)S(1)} all-to-all(bf16[2,2064,128]{2,1,0:T(8,128)(2,1)S(1)} %get-tuple-element.19), channel_id=1, replica_groups={{0,128},{256,384},{1,129},{257,385},{2,130},{258,386},{3,131},{259,387}..., dimensions={0} | all-to-all | bytes 2113536 | tf_op jit(solution)/shard_map/all_to_all | solution.py:502
  67.7 0.1 shard_map.121
  67.8 16.7 %all_to_all.26.received = bf16[4,528,128]{2,1,0:T(8,128)(2,1)S(1)} all-to-all(bf16[4,528,128]{2,1,0:T(8,128)(2,1)S(1)} %shard_map.121), channel_id=1, replica_groups={{0,8,16,24},{1,9,17,25},{2,10,18,26},{3,11,19,27},{4,12,20,28},{5,13,21..., dimensions={0} | all-to-all | bytes 1081344 | tf_op jit(solution)/shard_map/all_to_all | solution.py:508
  84.5 0.1 shard_map.122
  84.5 15.0 %all_to_all.27.received = bf16[8,80,128]{2,1,0:T(8,128)(2,1)S(1)} all-to-all(bf16[8,80,128]{2,1,0:T(8,128)(2,1)S(1)} %shard_map.122), channel_id=1, replica_groups={{0,1,2,3,4,5,6,7},{8,9,10,11,12,13,14,15},{16,17,18,19,20,21,22,23},{24..., dimensions={0} | all-to-all | bytes 327680 | tf_op jit(solution)/shard_map/all_to_all | solution.py:512
  99.5 26.7 %all_to_all.28.received = bf16[16,80,128]{2,1,0:T(8,128)(2,1)S(1)} all-to-all(bf16[16,80,128]{2,1,0:T(8,128)(2,1)S(1)} %shard_map.123), channel_id=1, replica_groups=mesh['gy'=4,'gx'=4,'dp'=32] {'gy','gx'}, dimensions={0} | all-to-all | bytes 655360 | tf_op jit(solution)/shard_map/all_to_all | solution.py:514
  126.2 0.7 shard_map.124
  (3 shorter events, 0.1 us)
Async XLA Ops:
  0.7 0.9 copy-start
  1.6 0.9 copy-start.1
  2.5 0.7 copy-start.2
  3.3 0.7 copy-start.3
  5.4 40.2 %copy-start.5 = (s32[1,4,4,2]{2,3,1,0:T(2,128)S(1)}, s32[1,4,4,2]{2,3,1,0:T(2,128)}, u32[]{:S(2)}) copy-start(s32[1,4,4,2]{2,3,1,0:T(2,128)} %param.8) | copy-start | bytes 388
  5.4 38.2 %all-to-all-start = ((bf16[32,64,128]{2,1,0:T(8,128)(2,1)}), bf16[32,64,128]{2,1,0:T(8,128)(2,1)S(1)}, u32[]{:S(2)}, u32[]{:S(2)}) async-start(bf16[32,64,128]{2,1,0:T(8,128)(2,1)} %get-tuple-element.16), calls=%async_computation | async-start | bytes 1048576 | tf_op jit(solution)/shard_map/all_to_all | solution.py:440
  16.1 29.7 %copy-start.6 = (f32[8,49]{1,0:T(8,128)S(1)}, f32[8,49]{1,0:T(8,128)}, u32[]{:S(2)}) copy-start(f32[8,49]{1,0:T(8,128)} %param.12) | copy-start | bytes 4708
  16.1 15.8 %collective-permute-start.1 = (bf16[128,1024]{1,0:T(8,128)(2,1)S(1)}, bf16[128,1024]{1,0:T(8,128)(2,1)S(1)}, u32[]{:S(2)}, u32[]{:S(2)}) collective-permute-start(bf16[128,1024]{1,0:T(8,128)(2,1)S(1)} %get-tuple-element.15), channel_id=1, source_target_pairs={{128,0},{256,128},{384,256},{129,1},{257,129},{385,257},{130,2},{2... | collective-permute-start | bytes 786440 | tf_op jit(solution)/shard_map/ppermute | solution.py:439
  19.0 19.3 %collective-permute-start = (bf16[128,1024]{1,0:T(8,128)(2,1)S(1)}, bf16[128,1024]{1,0:T(8,128)(2,1)S(1)}, u32[]{:S(2)}, u32[]{:S(2)}) collective-permute-start(bf16[128,1024]{1,0:T(8,128)(2,1)S(1)} %get-tuple-element.15), channel_id=1, source_target_pairs={{0,128},{128,256},{256,384},{1,129},{129,257},{257,385},{2,130},{1... | collective-permute-start | bytes 786440 | tf_op jit(solution)/shard_map/ppermute | solution.py:438
  38.3 12.7 %collective-permute-start.3 = (bf16[3,128,1024]{2,1,0:T(8,128)(2,1)S(1)}, bf16[3,128,1024]{2,1,0:T(8,128)(2,1)S(1)}, u32[]{:S(2)}, u32[]{:S(2)}) collective-permute-start(bf16[3,128,1024]{2,1,0:T(8,128)(2,1)S(1)} %pad_maximum_fusion.mid), channel_id=1, source_target_pairs={{32,0},{64,32},{96,64},{33,1},{65,33},{97,65},{34,2},{66,34},{98,6... | collective-permute-start | bytes 2359304 | tf_op jit(solution)/shard_map/ppermute | solution.py:443
  39.6 12.9 %collective-permute-start.2 = (bf16[3,128,1024]{2,1,0:T(8,128)(2,1)S(1)}, bf16[3,128,1024]{2,1,0:T(8,128)(2,1)S(1)}, u32[]{:S(2)}, u32[]{:S(2)}) collective-permute-start(bf16[3,128,1024]{2,1,0:T(8,128)(2,1)S(1)} %pad_maximum_fusion.mid), channel_id=1, source_target_pairs={{0,32},{32,64},{64,96},{1,33},{33,65},{65,97},{2,34},{34,66},{66,9... | collective-permute-start | bytes 2359304 | tf_op jit(solution)/shard_map/ppermute | solution.py:442
  43.7 8.9 %collective-permute-start.4 = (bf16[32,64,128]{2,1,0:T(8,128)(2,1)S(1)}, bf16[32,64,128]{2,1,0:T(8,128)(2,1)}, u32[]{:S(2)}, u32[]{:S(2)}) collective-permute-start(bf16[32,64,128]{2,1,0:T(8,128)(2,1)S(1)} %all-to-all-done.w_mine), channel_id=1, source_target_pairs={{0,128},{128,0},{256,384},{384,256},{1,129},{129,1},{257,385},{385... | collective-permute-start | bytes 1572872 | tf_op jit(solution)/shard_map/ppermute | solution.py:444
  45.9 6.6 %copy-start.4 = (f32[512]{0:T(512)S(1)}, f32[512]{0:T(512)}, u32[]{:S(2)}) copy-start(f32[512]{0:T(512)} %param.11) | copy-start | bytes 6148

commit v2 on v1

v2 whole, which is shorter than its diff:
```python
import functools

import jax
import jax.numpy as jnp
from jax import lax
from jax.experimental import pallas as pl
from jax.experimental.pallas import tpu as pltpu
from jax.sharding import PartitionSpec as P

D = 512
HEADS = 8
HD = 32
INNER = 256
TILE = 8
HALO = 3
REG = 4
CAP = 2
ROWS = 128
CELLS = TILE * TILE
DP = 32
NX = 4
NY = 8
PAIRS = 7
TILES = PAIRS * 2
BROWS = HEADS * CELLS
T_ROWS = 48
G_ROWS = 32
STRIP = T_ROWS + G_ROWS
MESSAGE = 2 * ROWS + 2 * STRIP
CHUNK = 128
FAR = 9
SCALE = HD ** (-0.5)
WROWS = 64
SMALL = 16
CORES = [[0, 1], [2, 3]]
XS = [[x * NY + y for x in range(NX)] for y in range(NY)]
YS = [[x * NY + y for y in range(NY)] for x in range(NX)]
ZS = [[0, 1, 2, 3, 8, 9, 10, 11], [4, 5, 6, 7, 12, 13, 14, 15]]
F32 = jnp.float32
BF = jnp.bfloat16
NT = (((1,), (1,)), ((), ()))
TN = (((0,), (0,)), ((), ()))
VM = pl.BlockSpec(memory_space=pltpu.VMEM)
SM = pl.BlockSpec(memory_space=pltpu.SMEM)
HBM = pl.BlockSpec(memory_space=pltpu.HBM)


def dot(a, b, dims=(((1,), (0,)), ((), ()))):
    return lax.dot_general(a, b, dims, preferred_element_type=F32)


def call(body, outs, ins, scratch=(), limit=16, flops=1000000, traffic=1000000):
    single = not isinstance(outs, (list, tuple))
    return pl.pallas_call(
        body,
        out_shape=outs,
        in_specs=ins,
        out_specs=VM if single else [VM] * len(outs),
        scratch_shapes=list(scratch),
        compiler_params=pltpu.CompilerParams(vmem_limit_bytes=limit * 2**20),
        cost_estimate=pl.CostEstimate(flops=flops, bytes_accessed=traffic, transcendentals=0),
    )


def shape(dims, dtype):
    return jax.ShapeDtypeStruct(dims, dtype)


def pack_body(wq_in, wo_in, tok_in, grad_in, w_out, rows, down, up, wq, wo, sems):
    copies = [
        pltpu.make_async_copy(wq_in, wq, sems.at[0]),
        pltpu.make_async_copy(wo_in, wo, sems.at[1]),
        pltpu.make_async_copy(tok_in, rows.at[pl.ds(0, ROWS)], sems.at[2]),
        pltpu.make_async_copy(grad_in, rows.at[pl.ds(ROWS, ROWS)], sems.at[3]),
    ]
    for copy in copies:
        copy.start()
    copies[0].wait()
    copies[1].wait()
    parts = []
    for c in range(2):
        parts += [wq[:, (3 * c + j) * 128 : (3 * c + j + 1) * 128].astype(F32) for j in range(3)]
        parts += [wo[:, (2 * c + j) * 128 : (2 * c + j + 1) * 128].astype(F32) for j in range(2)]
    block = jnp.concatenate(parts, axis=0).astype(BF)
    for d in range(DP):
        w_out[d] = block
    copies[2].wait()
    copies[3].wait()
    for s in range(CAP):
        t, g = s * CELLS, ROWS + s * CELLS
        down[s, 0:T_ROWS, :] = rows[t + CELLS - T_ROWS : t + CELLS, :]
        down[s, T_ROWS:STRIP, :] = rows[g + CELLS - G_ROWS : g + CELLS, :]
        up[s, 0:T_ROWS, :] = rows[t : t + T_ROWS, :]
        up[s, T_ROWS:STRIP, :] = rows[g : g + G_ROWS, :]


def corner_body(place, tiles, rows, above, below, to_right, to_left):
    over = jnp.maximum(place[0] - 1, 0)
    under = jnp.minimum(place[0] + 1, 3)
    col = place[1]
    for out, top, bottom in ((to_right, 15, 3), (to_left, 12, 0)):
        out[0 : 2 * ROWS, :] = rows[...]
        out[2 * ROWS : 2 * ROWS + STRIP, :] = above[
            (tiles[over, col, 1] == top).astype(jnp.int32)
        ]
        out[2 * ROWS + STRIP : MESSAGE, :] = below[
            (tiles[under, col, 1] == bottom).astype(jnp.int32)
        ]


def plan_tiles(place, tiles, plan, crow, ccol):
    my_row, my_col = place[0], place[1]
    steps = [(0, 0)] * 2 + [(-1, 0)] * 2 + [(1, 0)] * 2 + [(0, -1)] * 2 + [(0, 1)] * 2
    corners = [(-1, -1, 15), (-1, 1, 12), (1, -1, 3), (1, 1, 0)]
    for t, (dy, dx, *corner) in enumerate(steps + corners):
        ry, rx = my_row + dy, my_col + dx
        there = (ry >= 0) & (ry < 4) & (rx >= 0) & (rx < 4)
        ty, tx = jnp.clip(ry, 0, 3), jnp.clip(rx, 0, 3)
        if corner:
            tile = jnp.int32(corner[0])
            there = there & ((tiles[ty, tx, 0] == tile) | (tiles[ty, tx, 1] == tile))
        else:
            tile = tiles[ty, tx, t % 2]
        crow[t] = jnp.where(there, ry * REG + (tile >> 2), -1000 * (t + 1))
        ccol[t] = jnp.where(there, rx * REG + (tile & 3), -1000 * (t + 1))

    def near(a, b):
        return (jnp.abs(crow[a] - crow[b]) <= 1) & (jnp.abs(ccol[a] - ccol[b]) <= 1)

    def tile_plan(t, carry):
        plan[t, 0] = (near(t, 0) | near(t, 1)).astype(jnp.int32)
        count = jnp.int32(0)
        for r in range(PAIRS):
            plan[t, 2 + count] = r
            both = jnp.int32(0)
            for s in range(2):
                k = 2 * r + s
                close = near(t, k)
                down, across = crow[k] - crow[t], ccol[k] - ccol[t]
                plan[t, 10 + 8 * s + count] = jnp.where(close, down * 3 + across + 4, FAR)
                plan[t, 26 + 8 * s + count] = jnp.where(
                    close, (64 * down + 8 * across + 512) & 127, 0
                )
                both = both | close.astype(jnp.int32)
            count = count + both
        plan[t, 1] = count
        return carry

    lax.fori_loop(0, TILES, tile_plan, 0)


def table_body(place, tiles, base_ref, tab, plan, crow, ccol):
    plan_tiles(place, tiles, plan, crow, ccol)
    query = lax.broadcasted_iota(jnp.int32, (CELLS, 128), 0)
    lane = lax.broadcasted_iota(jnp.int32, (CELLS, 128), 1)
    key = lane & 63
    left = lane < 64
    row_step = (key >> 3) - (query >> 3)
    col_step = (key & 7) - (query & 7)
    base = base_ref[...]
    for place in range(9):
        down, across = place // 3 - 1, place % 3 - 1
        shift = 64 * down + 8 * across
        inside = (jnp.abs(row_step + 8 * down) <= HALO) & (jnp.abs(col_step + 8 * across) <= HALO)
        first = pltpu.roll(base, (-shift - 27) % 128, 1)
        second = pltpu.roll(base, (64 - shift - 27) % 128, 1)
        for h in range(HEADS):
            a = pltpu.roll(
                jnp.broadcast_to(first[h : h + 1], (CELLS, 128)), 0, 1, stride=1, stride_axis=0
            )
            b = pltpu.roll(
                jnp.broadcast_to(second[h : h + 1], (CELLS, 128)), 0, 1, stride=1, stride_axis=0
            )
            tab[place, h * CELLS : (h + 1) * CELLS, :] = jnp.where(
                inside, jnp.where(left, a, b), -jnp.inf
            )
    tab[FAR] = jnp.full((BROWS, 128), -jnp.inf, F32)


def prep_body(rows, above, below, left, right, gain, out):
    normed = out.at[pl.ds(0, PAIRS * ROWS)]
    grads = out.at[pl.ds(PAIRS * ROWS, PAIRS * ROWS)]
    own = out.at[pl.ds(2 * PAIRS * ROWS, ROWS)]
    gain_row = gain[...]

    def norm(block):
        x = block.astype(F32)
        inv = lax.rsqrt(jnp.mean(x * x, axis=-1, keepdims=True) + 1e-06)
        return (x * inv * gain_row).astype(BF)

    own[...] = rows[0:ROWS, :]
    for t, source in ((0, rows), (6, left), (8, right)):
        at = t * CELLS
        normed[at : at + ROWS, :] = norm(source[0:ROWS, :])
        grads[at : at + ROWS, :] = source[ROWS : 2 * ROWS, :]
    at_a, at_b = 2 * ROWS, 2 * ROWS + STRIP
    upper = [
        (2, above[0]),
        (3, above[1]),
        (10, left[at_a : at_a + STRIP, :]),
        (11, right[at_a : at_a + STRIP, :]),
    ]
    lower = [
        (4, below[0]),
        (5, below[1]),
        (12, left[at_b : at_b + STRIP, :]),
        (13, right[at_b : at_b + STRIP, :]),
    ]
    for t, strip in upper:
        at = t * CELLS
        normed[at : at + CELLS - T_ROWS, :] = jnp.zeros((CELLS - T_ROWS, D), BF)
        normed[at + CELLS - T_ROWS : at + CELLS, :] = norm(strip[0:T_ROWS])
        grads[at : at + CELLS - G_ROWS, :] = jnp.zeros((CELLS - G_ROWS, D), BF)
        grads[at + CELLS - G_ROWS : at + CELLS, :] = strip[T_ROWS:STRIP]
    for t, strip in lower:
        at = t * CELLS
        normed[at : at + T_ROWS, :] = norm(strip[0:T_ROWS])
        normed[at + T_ROWS : at + CELLS, :] = jnp.zeros((CELLS - T_ROWS, D), BF)
        grads[at : at + G_ROWS, :] = strip[T_ROWS:STRIP]
        grads[at + G_ROWS : at + CELLS, :] = jnp.zeros((CELLS - G_ROWS, D), BF)


def main_body(
    plan,
    packed,
    weights,
    gain,
    tab,
    update,
    grad_tokens,
    sums,
    wq,
    wo,
    qkv,
    gatt,
    qbd,
    gbd,
    scores,
    dprobs,
    top,
    total,
    delta,
    pbf,
    dsf,
    att,
    dq,
    attended,
    dqkv,
    dk,
    dv,
    hist,
    rowsum,
):
    normed = packed.at[pl.ds(0, PAIRS * ROWS)]
    grads = packed.at[pl.ds(PAIRS * ROWS, PAIRS * ROWS)]
    tokens = packed.at[pl.ds(2 * PAIRS * ROWS, ROWS)]
    for c in range(2):
        for j in range(3):
            at = WROWS * c + 16 * j
            wq[:, (3 * c + j) * 128 : (3 * c + j + 1) * 128] = weights[
                :, at : at + 16, :
            ].reshape(D, 128)
        both = weights[:, WROWS * c + 48 : WROWS * c + 64, :].astype(F32)
        for j in range(2):
            wo[:, (2 * c + j) * 128 : (2 * c + j + 1) * 128] = (
                both[:, 8 * j : 8 * j + 8, :].reshape(INNER, 128).astype(BF)
            )

    gain_row = gain[...]
    for j in range(3):
        cols = slice(j * INNER, (j + 1) * INNER)
        qkv[:, cols] = dot(normed[...], wq[:, cols]).astype(BF)
    gatt[...] = dot(grads[...], wo[...], NT).astype(BF)

    dk[...] = jnp.zeros_like(dk)
    dv[...] = jnp.zeros_like(dv)
    hist[...] = jnp.zeros_like(hist)
    head_of = lax.broadcasted_iota(jnp.int32, (1, INNER), 1) >> 5
    masks_bf = [(head_of == h).astype(F32).astype(BF) for h in range(HEADS)]
    lane = lax.broadcasted_iota(jnp.int32, (CHUNK, 128), 1)
    first_slot = lane < 64
    lane_masks = [((lane[0:CELLS] >> 5) == h).astype(F32) for h in range(4)]
    mirror = ((lane + lax.broadcasted_iota(jnp.int32, (128, 128), 0)) == 127).astype(F32)
    mirror_bf = mirror.astype(BF)

    def process(i, own, q_at, nq):
        per = CHUNK // nq
        chunks = HEADS // per
        used = HEADS * nq
        at = pl.multiple_of(i * CELLS, CELLS) + q_at
        queries = qkv[pl.ds(at, nq), 0:INNER]
        cotangents = gatt[pl.ds(at, nq), :]
        for h in range(HEADS):
            qbd[h * nq : (h + 1) * nq, :] = queries * masks_bf[h]
            gbd[h * nq : (h + 1) * nq, :] = cotangents * masks_bf[h]
        count = plan[i, 1]

        def bias_of(off, c):
            parts = [
                tab[off, (c * per + h) * CELLS + q_at : (c * per + h) * CELLS + q_at + nq, :]
                for h in range(per)
            ]
            return jnp.concatenate(parts, axis=0)

        def pass_a(b, first):
            k_at = pl.multiple_of(plan[i, 2 + b] * ROWS, ROWS)
            keys = qkv[pl.ds(k_at, ROWS), INNER : 2 * INNER]
            values = qkv[pl.ds(k_at, ROWS), 2 * INNER : 3 * INNER]
            off_a, off_b = plan[i, 10 + b], plan[i, 18 + b]
            scores[b, 0:used, :] = dot(qbd[0:used, :], keys, NT)
            dprobs[b, 0:used, :] = dot(gbd[0:used, :], values, NT)
            for c in range(chunks):
                rows = slice(c * CHUNK, (c + 1) * CHUNK)
                bias = jnp.where(first_slot, bias_of(off_a, c), bias_of(off_b, c))
                s = scores[b, rows, :] * SCALE + bias
                scores[b, rows, :] = s
                top[rows, :] = s if first else jnp.maximum(top[rows, :], s)

        def rest_a(b, carry):
            pass_a(b, False)
            return carry

        pass_a(0, True)
        lax.fori_loop(1, count, rest_a, 0)
        for c in range(chunks):
            rows = slice(c * CHUNK, (c + 1) * CHUNK)
            top[rows, :] = jnp.broadcast_to(
                jnp.max(top[rows, :], axis=-1, keepdims=True), (CHUNK, 128)
            )

        def pass_b(b, first):
            for c in range(chunks):
                rows = slice(c * CHUNK, (c + 1) * CHUNK)
                e = jnp.exp(scores[b, rows, :] - top[rows, :])
                d = e * dprobs[b, rows, :]
                scores[b, rows, :] = e
                total[rows, :] = e if first else total[rows, :] + e
                delta[rows, :] = d if first else delta[rows, :] + d

        def rest_b(b, carry):
            pass_b(b, False)
            return carry

        pass_b(0, True)
        lax.fori_loop(1, count, rest_b, 0)
        for c in range(chunks):
            rows = slice(c * CHUNK, (c + 1) * CHUNK)
            inverse = 1.0 / jnp.sum(total[rows, :], axis=-1, keepdims=True)
            d = jnp.sum(delta[rows, :], axis=-1, keepdims=True) * inverse
            total[rows, :] = jnp.broadcast_to(inverse, (CHUNK, 128))
            delta[rows, :] = jnp.broadcast_to(d, (CHUNK, 128))

        def probs_of(b):
            for c in range(chunks):
                rows = slice(c * CHUNK, (c + 1) * CHUNK)
                p = scores[b, rows, :] * total[rows, :]
                pbf[rows, :] = p.astype(BF)
                dsf[rows, :] = (p * (dprobs[b, rows, :] - delta[rows, :])).astype(BF)

        def pass_c(b, first):
            k_at = pl.multiple_of(plan[i, 2 + b] * ROWS, ROWS)
            keys = qkv[pl.ds(k_at, ROWS), INNER : 2 * INNER]
            values = qkv[pl.ds(k_at, ROWS), 2 * INNER : 3 * INNER]
            probs_of(b)
            for sum_ref, factor, other in ((att, pbf, values), (dq, dsf, keys)):
                wide = dot(factor[...], other)
                for n in range(2):
                    cols = slice(n * 128, (n + 1) * 128)
                    acc = None if first else sum_ref[:, cols]
                    for h in range(4 * n, 4 * n + 4):
                        part = wide[h * CELLS : (h + 1) * CELLS, cols] * lane_masks[h & 3]
                        acc = part if acc is None else acc + part
                    sum_ref[:, cols] = acc
            flipped = dot(dsf[...], mirror_bf)
            half = first_slot[0:CELLS]
            for h in range(HEADS):
                ds = flipped[h * CELLS : (h + 1) * CELLS]
                for s, part in enumerate((jnp.where(half, 0.0, ds), jnp.where(half, ds, 0.0))):
                    turned = pltpu.roll(part, 0, 1, stride=1, stride_axis=0)
                    rowsum[s, h : h + 1, :] = jnp.sum(turned, axis=0, keepdims=True)
            for s in range(2):
                shift = (64 * s - 27 - plan[i, 26 + 8 * s + b] + 256) & 127
                hist[...] += pltpu.roll(rowsum[s], shift, 1)

        def rest_c(b, carry):
            pass_c(b, False)
            return carry

        if own:
            pass_c(0, True)
        else:
            probs_of(0)
        dk[...] += dot(dsf[0:used, :], qbd[0:used, :], TN)
        dv[...] += dot(pbf[0:used, :], gbd[0:used, :], TN)
        if own:
            lax.fori_loop(1, count, rest_c, 0)
            slot_at = pl.multiple_of(i * CELLS, CELLS)
            attended[pl.ds(slot_at, CELLS), :] = att[...].astype(BF)
            dqkv[pl.ds(slot_at, CELLS), 0:INNER] = (dq[...] * SCALE).astype(BF)

    def own_step(s, carry):
        process(s, True, 0, CELLS)
        return carry

    lax.fori_loop(0, 2, own_step, 0)

    def others(tile_of, q_at, nq):
        def step(n, carry):
            t = tile_of(n)
            pl.when(plan[t, 0] > 0)(lambda: process(t, False, q_at, nq))
            return carry

        lax.fori_loop(0, 4, step, 0)

    others(lambda n: n + 6, 0, CELLS)
    others(lambda n: n + jnp.where(n < 2, 2, 8), CELLS - G_ROWS, G_ROWS)
    others(lambda n: n + jnp.where(n < 2, 4, 10), 0, G_ROWS)

    dqkv[:, INNER : 2 * INNER] = (dk[...] * SCALE).astype(BF)
    dqkv[:, 2 * INNER : 3 * INNER] = dv[...].astype(BF)
    update[...] = dot(attended[...], wo[...]).astype(BF)
    grad_out = dot(attended[...], grads[0:ROWS, :], TN)
    for c in range(2):
        pair = [
            grad_out[:, (2 * c + j) * 128 : (2 * c + j + 1) * 128].reshape(DP, 8, 128)
            for j in range(2)
        ]
        both = jnp.concatenate(pair, axis=1).astype(BF)
        for d in range(DP):
            sums[c, d * WROWS + 48 : d * WROWS + 64, :] = both[d]
    for n in range(3):
        pair = dot(normed[0:ROWS, :], dqkv[:, n * 256 : (n + 1) * 256], TN).astype(BF)
        for j in (2 * n, 2 * n + 1):
            block = pair[:, (j - 2 * n) * 128 : (j - 2 * n + 1) * 128]
            for d in range(DP):
                at = d * WROWS + (j % 3) * 16
                sums[j // 3, at : at + 16, :] = block[d * 16 : (d + 1) * 16]
    d_normed = dot(dqkv[...], wq[...], NT)
    x = tokens[...].astype(F32)
    inv = lax.rsqrt(jnp.mean(x * x, axis=-1, keepdims=True) + 1e-06)
    scaled = d_normed * gain_row
    gain_sum = jnp.sum(d_normed * x * inv, axis=0, keepdims=True)
    grad_tokens[...] = (
        inv * scaled - x * (inv * inv * inv) * jnp.mean(scaled * x, axis=-1, keepdims=True)
    ).astype(BF)
    offsets = lax.dot_general(
        hist[...],
        mirror,
        (((1,), (0,)), ((), ())),
        precision=lax.Precision.HIGHEST,
        preferred_element_type=F32,
    )
    folded = offsets[0:4, :] + pltpu.roll(offsets[4:8, :], 64, 1)
    small = jnp.concatenate([gain_sum[:, j * 128 : (j + 1) * 128] for j in range(4)] + [folded], 0)
    split = halves(small)
    sums[0, DP * WROWS : DP * WROWS + SMALL, :] = split
    sums[1, DP * WROWS : DP * WROWS + SMALL, :] = split


def halves(value):
    high = value.astype(BF).astype(F32)
    return jnp.concatenate([high, value - high], axis=0).astype(BF)


def whole(value):
    wide = value.astype(F32)
    return wide[..., 0:8, :] + wide[..., 8:16, :]


def sum_body(senders, parts, span, received, out):
    rows = parts * span
    for p in range(parts):
        acc = received[0, p * span : (p + 1) * span, :].astype(F32)
        for s in range(1, senders):
            acc += received[s, p * span : (p + 1) * span, :].astype(F32)
        out[p, 0:span, :] = acc.astype(BF)
    small = whole(received[0, rows : rows + SMALL, :])
    for s in range(1, senders):
        small += whole(received[s, rows : rows + SMALL, :])
    split = halves(small)
    for p in range(parts):
        out[p, span : span + SMALL, :] = split


def last_sum_body(received, out):
    acc = received[0, 0:WROWS, :].astype(F32)
    small = whole(received[0, WROWS : WROWS + SMALL, :])
    for s in range(1, NY):
        acc += received[s, 0:WROWS, :].astype(F32)
        small += whole(received[s, WROWS : WROWS + SMALL, :])
    acc = acc.astype(BF)
    split = halves(small)
    for p in range(8):
        out[p, 0:WROWS, :] = acc
        out[p, WROWS : WROWS + SMALL, :] = split


def z_body(received, mine, small):
    acc = received[0, 0:WROWS, :].astype(F32)
    more = whole(received[0, WROWS : WROWS + SMALL, :])
    for s in range(1, 8):
        acc += received[s, 0:WROWS, :].astype(F32)
        more += whole(received[s, WROWS : WROWS + SMALL, :])
    mine[...] = acc.astype(BF)
    small[...] = more


def finish_body(place, mine, theirs, small_in, grad_qkv, grad_out, grad_gain, grad_bias):
    small = small_in[...]
    odd = place[0] & 1

    def unpack(pair):
        for c, ref in enumerate(pair):
            acc = ref[...].astype(F32)
            for j in range(3):
                at = (3 * c + j) * 128
                grad_qkv[:, at : at + 128] = acc[16 * j : 16 * j + 16, :]
            for j in range(2):
                at = 48 + 8 * j
                grad_out[:, (2 * c + j) * 128 : (2 * c + j + 1) * 128] = acc[at : at + 8, :]

    pl.when(odd == 0)(lambda: unpack((mine, theirs)))
    pl.when(odd == 1)(lambda: unpack((theirs, mine)))
    for j in range(4):
        grad_gain[:, j * 128 : (j + 1) * 128] = small[j : j + 1, :]
    folded = small[4:8, :]
    table = jnp.concatenate([folded, pltpu.roll(folded, 64, 1)], axis=0)
    lane = lax.broadcasted_iota(jnp.int32, (HEADS, 128), 1)
    out = jnp.zeros((HEADS, 128), F32)
    for r in range(7):
        moved = table if r == 0 else pltpu.roll(table, 128 - r, 1)
        out = jnp.where((lane >= 7 * r) & (lane < 7 * r + 7), moved, out)
    grad_bias[...] = out[:, 0:49]


def layer(plan, packed, weights, gain, table):
    f32 = lambda *dims: pltpu.VMEM(dims, F32)
    bf = lambda *dims: pltpu.VMEM(dims, BF)
    return call(
        main_body,
        [
            shape((ROWS, D), BF),
            shape((ROWS, D), BF),
            shape((2, DP * WROWS + SMALL, 128), BF),
        ],
        [SM] + [VM] * 4,
        [
            bf(D, 3 * INNER),
            bf(INNER, D),
            bf(PAIRS * ROWS, 3 * INNER),
            bf(PAIRS * ROWS, INNER),
            bf(BROWS, INNER),
            bf(BROWS, INNER),
            f32(4, BROWS, 128),
            f32(4, BROWS, 128),
            f32(BROWS, 128),
            f32(BROWS, 128),
            f32(BROWS, 128),
            bf(BROWS, 128),
            bf(BROWS, 128),
            f32(CELLS, INNER),
            f32(CELLS, INNER),
            bf(ROWS, INNER),
            bf(ROWS, 3 * INNER),
            f32(ROWS, INNER),
            f32(ROWS, INNER),
            f32(HEADS, 128),
            f32(CAP, HEADS, 128),
        ],
        limit=40,
        flops=4000000000,
        traffic=12000000,
    )(plan, packed, weights, gain, table)


def shards(tokens, tile_ids, w_qkv, w_out, norm_gain, rel_bias, update_grad):
    my_row = lax.axis_index("gy")
    my_col = lax.axis_index("gx")
    place = jnp.stack([my_row, my_col]).astype(jnp.int32)
    forth = [(0, 1), (1, 2), (2, 3)]
    back = [(1, 0), (2, 1), (3, 2)]

    tiles = tile_ids.reshape(4, 4, CAP)
    strip = shape((CAP, STRIP, D), BF)
    w_send, rows, down, up = call(
        pack_body,
        [shape((DP, 2 * WROWS, 128), BF), shape((2 * ROWS, D), BF), strip, strip],
        [HBM, HBM, HBM, HBM],
        [
            pltpu.VMEM((16, 3 * INNER), BF),
            pltpu.VMEM((8, D), BF),
            pltpu.SemaphoreType.DMA((4,)),
        ],
        limit=60,
    )(w_qkv, w_out, tokens.reshape(ROWS, D), update_grad.reshape(ROWS, D))
    above = lax.ppermute(down, "gy", forth)
    below = lax.ppermute(up, "gy", back)
    weights = lax.all_to_all(w_send, "dp", 0, 0, tiled=True)
    message = shape((MESSAGE, D), BF)
    to_right, to_left = call(corner_body, [message, message], [SM, SM, VM, VM, VM], flops=16000000000)(
        place, tiles, rows, above, below
    )
    left = lax.ppermute(to_right, "gx", forth)
    right = lax.ppermute(to_left, "gx", back)
    base = jnp.pad(rel_bias.reshape(HEADS, 7, 7), ((0, 0), (0, 0), (0, 1))).reshape(HEADS, 56)
    base = jnp.pad(base, ((0, 0), (0, 72)))
    table, plan = pl.pallas_call(
        table_body,
        out_shape=[shape((10, BROWS, 128), F32), shape((TILES, 48), jnp.int32)],
        in_specs=[SM, SM, VM],
        out_specs=[VM, SM],
        scratch_shapes=[pltpu.SMEM((TILES,), jnp.int32), pltpu.SMEM((TILES,), jnp.int32)],
        compiler_params=pltpu.CompilerParams(vmem_limit_bytes=16 * 2**20),
        cost_estimate=pl.CostEstimate(flops=2000000, bytes_accessed=4000000, transcendentals=0),
    )(place, tiles, base)
    packed = call(prep_body, shape((2 * PAIRS * ROWS + ROWS, D), BF), [VM] * 6)(
        rows, above, below, left, right, norm_gain.reshape(1, D)
    )
    update, grad_tokens, sums = layer(plan, packed, weights, norm_gain.reshape(1, D), table)

    got = lax.all_to_all(sums, "gy", 0, 0, tiled=True, axis_index_groups=CORES)
    got = call(
        functools.partial(sum_body, 2, NX, NY * WROWS),
        shape((NX, NY * WROWS + SMALL, 128), BF),
        [VM],
    )(got)
    got = lax.all_to_all(got, "dp", 0, 0, tiled=True, axis_index_groups=XS)
    got = call(
        functools.partial(sum_body, NX, NY, WROWS), shape((NY, WROWS + SMALL, 128), BF), [VM]
    )(got)
    got = lax.all_to_all(got, "dp", 0, 0, tiled=True, axis_index_groups=YS)
    got = call(last_sum_body, shape((8, WROWS + SMALL, 128), BF), [VM])(got)
    got = lax.all_to_all(got, ("gy", "gx"), 0, 0, tiled=True, axis_index_groups=ZS)
    mine, small = call(z_body, [shape((WROWS, 128), BF), shape((8, 128), F32)], [VM])(got)
    theirs = lax.ppermute(mine, "gy", [(0, 1), (1, 0), (2, 3), (3, 2)])
    grad_qkv, grad_out, grad_gain, grad_bias = call(
        finish_body,
        [
            shape((16, 3 * INNER), F32),
            shape((8, D), F32),
            shape((1, D), F32),
            shape((HEADS, 49), F32),
        ],
        [SM, VM, VM, VM],
    )(place, mine, theirs, small)
    return (
        update.reshape(tokens.shape),
        grad_tokens.reshape(tokens.shape),
        grad_qkv,
        grad_out,
        grad_gain.reshape(D),
        grad_bias,
    )


def solution(mesh):
    return jax.shard_map(
        shards,
        mesh=mesh,
        in_specs=(
            P("dp", "gy", "gx", None, None),
            P("dp", None, None, None),
            P("dp", None),
            P("dp", None),
            P(),
            P(),
            P("dp", "gy", "gx", None, None),
        ),
        out_specs=(
            P("dp", "gy", "gx", None, None),
            P("dp", "gy", "gx", None, None),
            P("dp", None),
            P("dp", None),
            P(),
            P(),
        ),
        check_vma=False,
    )
```

time: 128 us -> 116 us (0.906)
  waiting for transfers between devices: 14.7 us -> 3.79 us
  blocking collectives: 62.5 us -> 53.5 us
  local copies, waits for them, and re-layouts: 3.53 us -> 8.08 us
  starting transfers between devices: 31.3 us -> 34 us
  Pallas kernels: 14.1 us -> 15.5 us
    ppermute x5, waiting for transfers between devices: 14.7 us -> 2.56 us  [the longest x1 1.73 us: shards(): right = lax.ppermute(to_left, 'gx', back)]
    all_to_all x1, blocking collectives: 26.7 us -> 19.6 us  [shards(): lax.all_to_all(got, ('gy', 'gx'), 0, 0, tiled=True, axis_index_groups=ZS)]
    unnamed x14 -> x26, local copies, waits for them, and re-layouts: 3.26 us -> 7.8 us
    ppermute x5, starting transfers between devices: 20.6 us -> 24.3 us  [the longest x1 12.2 us: shards(): above = lax.ppermute(down, 'gy', forth)]
    all_to_all x1, blocking collectives: 16.7 us -> 13.5 us  [shards(): got = lax.all_to_all(got, 'dp', 0, 0, tiled=True, axis_index_groups=XS)]
    pallas_call x4 -> x7, Pallas kernels: 13.1 us -> 14 us  [the longest x1 5.77 us: layer(): call(main_body, [shape((ROWS, D), BF), shape((ROWS, D), BF), shape((2, DP...]
  transfers between devices with their start and end apart: 6 -> 6, of which waited for: 4 -> 3; matrix products, arithmetic and copies ran while one was open for 0% -> 0% of each run, Pallas kernels for 1% -> 5%
where the time goes in v2:
time: 116 us
  blocking collectives  53.5 us (46%)
  starting transfers between devices  34 us (29%)
  Pallas kernels  15.5 us (13%)
  local copies, waits for them, and re-layouts  8.08 us (7%)
  waiting for transfers between devices  3.79 us (3%)
    all_to_all x1, blocking collectives, shards(): lax.all_to_all(got, ('gy', 'gx'), 0, 0, tiled=True, axis_index_groups=ZS)  19.6 us
    all_to_all x1, blocking collectives, shards(): got = lax.all_to_all(got, 'dp', 0, 0, tiled=True, axis_index_groups=YS)  16.2 us
    all_to_all x1, blocking collectives, shards(): got = lax.all_to_all(got, 'dp', 0, 0, tiled=True, axis_index_groups=XS)  13.5 us
    ppermute x1, starting transfers between devices, shards(): above = lax.ppermute(down, 'gy', forth)  12.2 us
    all_to_all x1, starting transfers between devices, shards(): weights = lax.all_to_all(w_send, 'dp', 0, 0, tiled=True)  9.68 us
    unnamed x26, local copies, waits for them, and re-layouts  7.8 us
    ppermute x1, starting transfers between devices, shards(): theirs = lax.ppermute(mine, 'gy', [(0, 1), (1, 0), (2, 3), (3, 2)])  5.82 us
    pallas_call x1, Pallas kernels, layer(): call(main_body, [shape((ROWS, D), BF), shape((ROWS, D), BF), shape((2, DP...  5.77 us
  transfers between devices with their start and end apart: 6, of which 3 were waited for; matrix products, arithmetic and copies ran while one was open for 0% of the time, Pallas kernels for 5%

profile of v2, /device:TPU:1, one launch (start us, length us, event | category | flops | bytes accessed | tf_op | source)
XLA Modules:
  0.0 115.7 jit_solution(2310526754929895716)
XLA Ops:
  0.6 0.0 copy-start.11
  0.6 2.2 %shard_map.119 = (bf16[32,128,128]{2,1,0:T(8,128)(2,1)}, bf16[256,512]{1,0:T(8,128)(2,1)}, bf16[2,80,512]{2,1,0:T(8,128)(2,1)}, bf16[2,80,512]{2,1,0:T(8,128)(2,1)}) custom-call(bf16[16,768]{1,0:T(8,128)(2,1)} %wq_in.1, bf16[8,512]{1,0:T(8,128)(2,1)} %wo_in.1, bf16[128,512]{1,0:T(8,128)(2,1)} %bitcast.11, bf16[128,512]{1,0:T(8,128)(2,1)} %bitcast.12), custom_call_target="tpu_custom_call" | custom-call | flops 1000000 | bytes 1000000 | tf_op jit(solution)/shard_map/pallas_call | solution.py:585
  2.9 0.0 copy-start.2
  2.9 12.2 %collective-permute-start = (bf16[2,80,512]{2,1,0:T(8,128)(2,1)}, bf16[2,80,512]{2,1,0:T(8,128)(2,1)S(1)}, u32[]{:S(2)}, u32[]{:S(2)}) collective-permute-start(bf16[2,80,512]{2,1,0:T(8,128)(2,1)} %get-tuple-element.25), channel_id=1, source_target_pairs={{0,128},{128,256},{256,384},{1,129},{129,257},{257,385},{2,130},{1... | collective-permute-start | bytes 491528 | tf_op jit(solution)/shard_map/ppermute | solution.py:596
  15.1 1.9 %collective-permute-start.1 = (bf16[2,80,512]{2,1,0:T(8,128)(2,1)}, bf16[2,80,512]{2,1,0:T(8,128)(2,1)S(1)}, u32[]{:S(2)}, u32[]{:S(2)}) collective-permute-start(bf16[2,80,512]{2,1,0:T(8,128)(2,1)} %get-tuple-element.26), channel_id=1, source_target_pairs={{128,0},{256,128},{384,256},{129,1},{257,129},{385,257},{130,2},{2... | collective-permute-start | bytes 491528 | tf_op jit(solution)/shard_map/ppermute | solution.py:597
  17.0 9.7 %all-to-all-start = ((bf16[32,128,128]{2,1,0:T(8,128)(2,1)}), bf16[32,128,128]{2,1,0:T(8,128)(2,1)S(1)}, u32[]{:S(2)}, u32[]{:S(2)}) async-start(bf16[32,128,128]{2,1,0:T(8,128)(2,1)} %get-tuple-element.29), calls=%async_computation | async-start | bytes 2097152 | tf_op jit(solution)/shard_map/all_to_all | solution.py:598
  26.7 0.0 copy-done.11
  26.7 0.1 copy.17.tiles
  26.8 0.1 pad_add_fusion.place
  26.9 0.0 collective-permute-done.above
  26.9 0.0 copy-start.4
  26.9 0.0 collective-permute-done.1.below
  26.9 0.0 copy-start.6
  26.9 0.0 copy-done.2
  26.9 0.0 copy-start.12
  26.9 0.0 copy-start.8
  26.9 0.7 shard_map.120
  27.7 0.0 copy-done.4
  27.7 0.0 copy-done.6
  27.7 3.1 %collective-permute-start.2 = (bf16[416,512]{1,0:T(8,128)(2,1)S(1)}, bf16[416,512]{1,0:T(8,128)(2,1)S(1)}, u32[]{:S(2)}, u32[]{:S(2)}) collective-permute-start(bf16[416,512]{1,0:T(8,128)(2,1)S(1)} %get-tuple-element.27), channel_id=1, source_target_pairs={{0,32},{32,64},{64,96},{1,33},{33,65},{65,97},{2,34},{34,66},{66,9... | collective-permute-start | bytes 1277960 | tf_op jit(solution)/shard_map/ppermute | solution.py:603
  30.8 1.3 %collective-permute-start.3 = (bf16[416,512]{1,0:T(8,128)(2,1)S(1)}, bf16[416,512]{1,0:T(8,128)(2,1)S(1)}, u32[]{:S(2)}, u32[]{:S(2)}) collective-permute-start(bf16[416,512]{1,0:T(8,128)(2,1)S(1)} %get-tuple-element.28), channel_id=1, source_target_pairs={{32,0},{64,32},{96,64},{33,1},{65,33},{97,65},{34,2},{66,34},{98,6... | collective-permute-start | bytes 1277960 | tf_op jit(solution)/shard_map/ppermute | solution.py:604
  32.1 0.0 copy-done.12
  32.1 0.1 reshape.41
  32.2 0.1 reshape.42
  32.3 4.8 %shard_map.118 = (f32[10,512,128]{2,1,0:T(8,128)S(1)}, s32[14,48]{1,0:T(8,128)S(1)}) custom-call(s32[2]{0:T(128)S(1)} %pad_add_fusion.place, s32[4,4,2]{2,1,0:T(4,128)S(1)} %copy.17.tiles, f32[8,128]{1,0:T(8,128)S(1)} %pad.9.base_ref), custom_call_target="tpu_custom_call" | custom-call | flops 2000000 | bytes 4000000 | tf_op jit(solution)/shard_map/pallas_call | solution.py:607
  37.1 0.0 copy-start.9
  37.1 1.5 %copy-done.9 = f32[10,512,128]{2,1,0:T(8,128)} copy-done((f32[10,512,128]{2,1,0:T(8,128)}, f32[10,512,128]{2,1,0:T(8,128)S(1)}, u32[]{:S(2)}) %copy-start.9) | copy-done | bytes 2621464
  38.6 0.0 collective-permute-done.2.left
  38.6 1.7 %collective-permute-done.3.right = bf16[416,512]{1,0:T(8,128)(2,1)S(1)} collective-permute-done((bf16[416,512]{1,0:T(8,128)(2,1)S(1)}, bf16[416,512]{1,0:T(8,128)(2,1)S(1)}, u32[]{:S(2)}, u32[]{:S(2)}) %collective-permute-start.3) | collective-permute-done | bytes 426016 | tf_op jit(solution)/shard_map/ppermute | solution.py:604
  40.4 0.0 copy-start
  40.4 0.8 copy-done
  41.1 0.0 copy-done.8
  41.1 0.0 copy-start.1
  41.1 1.0 copy-done.1
  42.1 0.0 copy-start.3
  42.1 0.9 copy-done.3
  43.1 0.0 copy-start.5
  43.1 0.9 copy-done.5
  44.0 0.0 copy-start.7
  44.0 0.9 copy-done.7
  44.9 0.4 shard_map.121.packed
  45.3 1.2 %all-to-all-done.weights = bf16[32,128,128]{2,1,0:T(8,128)(2,1)S(1)} async-done(((bf16[32,128,128]{2,1,0:T(8,128)(2,1)}), bf16[32,128,128]{2,1,0:T(8,128)(2,1)S(1)}, u32[]{:S(2)}, u32[]{:S(2)}) %all-to-all-start) | async-done | bytes 1048608 | tf_op jit(solution)/shard_map/all_to_all | solution.py:598
  46.5 0.0 copy-start.10
  46.5 1.7 %copy-done.10 = f32[10,512,128]{2,1,0:T(8,128)S(1)} copy-done((f32[10,512,128]{2,1,0:T(8,128)S(1)}, f32[10,512,128]{2,1,0:T(8,128)}, u32[]{:S(2)}) %copy-start.10) | copy-done | bytes 2621464
  48.2 5.8 %shard_map.122 = (bf16[128,512]{1,0:T(8,128)(2,1)}, bf16[128,512]{1,0:T(8,128)(2,1)}, bf16[2,2064,128]{2,1,0:T(8,128)(2,1)S(1)}) custom-call(s32[14,48]{1,0:T(8,128)S(1)} %get-tuple-element.23.plan, bf16[1920,512]{1,0:T(8,128)(2,1)S(1)} %shard_map.121.packed, bf16[32,128,128]{2,1,0:T(8,128)(2,1)S(1)} %all-to-all-done.weights, f32[1,512]{1,0:T(1,128)S(1)} %bitcast.10, ...), custom_call_target="tpu_custom_call" | custom-call | flops 4000000000 | bytes 12000000 | tf_op jit(solution)/shard_map/pallas_call | solution.py:539
  54.0 4.2 %all_to_all.25.received = bf16[2,2064,128]{2,1,0:T(8,128)(2,1)S(1)} all-to-all(bf16[2,2064,128]{2,1,0:T(8,128)(2,1)S(1)} %get-tuple-element.33), channel_id=1, replica_groups={{0,128},{256,384},{1,129},{257,385},{2,130},{258,386},{3,131},{259,387}..., dimensions={0} | all-to-all | bytes 2113536 | tf_op jit(solution)/shard_map/all_to_all | solution.py:621
  58.2 0.1 shard_map.123
  58.3 13.5 %all_to_all.26.received = bf16[4,528,128]{2,1,0:T(8,128)(2,1)S(1)} all-to-all(bf16[4,528,128]{2,1,0:T(8,128)(2,1)S(1)} %shard_map.123), channel_id=1, replica_groups={{0,8,16,24},{1,9,17,25},{2,10,18,26},{3,11,19,27},{4,12,20,28},{5,13,21..., dimensions={0} | all-to-all | bytes 1081344 | tf_op jit(solution)/shard_map/all_to_all | solution.py:627
  71.8 0.1 shard_map.124
  71.9 16.2 %all_to_all.27.received = bf16[8,80,128]{2,1,0:T(8,128)(2,1)S(1)} all-to-all(bf16[8,80,128]{2,1,0:T(8,128)(2,1)S(1)} %shard_map.124), channel_id=1, replica_groups={{0,1,2,3,4,5,6,7},{8,9,10,11,12,13,14,15},{16,17,18,19,20,21,22,23},{24..., dimensions={0} | all-to-all | bytes 327680 | tf_op jit(solution)/shard_map/all_to_all | solution.py:631
  88.1 19.6 %all_to_all.28.received = bf16[8,80,128]{2,1,0:T(8,128)(2,1)S(1)} all-to-all(bf16[8,80,128]{2,1,0:T(8,128)(2,1)S(1)} %shard_map.125), channel_id=1, replica_groups={{0,32,64,96,256,288,320,352},{128,160,192,224,384,416,448,480},{1,33,65..., dimensions={0} | all-to-all | bytes 327680 | tf_op jit(solution)/shard_map/all_to_all | solution.py:633
  107.7 5.8 %collective-permute-start.4 = (bf16[64,128]{1,0:T(8,128)(2,1)S(1)}, bf16[64,128]{1,0:T(8,128)(2,1)S(1)}, u32[]{:S(2)}, u32[]{:S(2)}) collective-permute-start(bf16[64,128]{1,0:T(8,128)(2,1)S(1)} %get-tuple-element.34.mine), channel_id=1, source_target_pairs={{0,128},{128,0},{256,384},{384,256},{1,129},{129,1},{257,385},{385... | collective-permute-start | bytes 49160 | tf_op jit(solution)/shard_map/ppermute | solution.py:635
  113.6 0.8 collective-permute-done.4.theirs
  114.4 1.3 %shard_map.127 = (f32[16,768]{1,0:T(8,128)}, f32[8,512]{1,0:T(8,128)}, f32[1,512]{1,0:T(1,128)}, f32[8,49]{1,0:T(8,128)}) custom-call(s32[2]{0:T(128)S(1)} %pad_add_fusion.place, bf16[64,128]{1,0:T(8,128)(2,1)S(1)} %get-tuple-element.34.mine, bf16[64,128]{1,0:T(8,128)(2,1)S(1)} %collective-permute-done.4.theirs, f32[8,128]{1,0:T(8,128)S(1)} %get-tuple-element.35.small_in), custom_call_target="tpu_custom_call" | custom-call | flops 1000000 | bytes 1000000 | tf_op jit(solution)/shard_map/pallas_call | solution.py:636
  (4 shorter events, 0.1 us)
Async XLA Ops:
  0.6 26.1 %copy-start.11 = (s32[1,4,4,2]{2,3,1,0:T(2,128)S(1)}, s32[1,4,4,2]{2,3,1,0:T(2,128)}, u32[]{:S(2)}) copy-start(s32[1,4,4,2]{2,3,1,0:T(2,128)} %param.8) | copy-start | bytes 388
  2.9 24.0 %copy-start.2 = (bf16[256,512]{1,0:T(8,128)(2,1)S(1)}, bf16[256,512]{1,0:T(8,128)(2,1)}, u32[]{:S(2)}) copy-start(bf16[256,512]{1,0:T(8,128)(2,1)} %get-tuple-element.24.rows) | copy-start | bytes 786436
  2.9 24.0 %collective-permute-start = (bf16[2,80,512]{2,1,0:T(8,128)(2,1)}, bf16[2,80,512]{2,1,0:T(8,128)(2,1)S(1)}, u32[]{:S(2)}, u32[]{:S(2)}) collective-permute-start(bf16[2,80,512]{2,1,0:T(8,128)(2,1)} %get-tuple-element.25), channel_id=1, source_target_pairs={{0,128},{128,256},{256,384},{1,129},{129,257},{257,385},{2,130},{1... | collective-permute-start | bytes 491528 | tf_op jit(solution)/shard_map/ppermute | solution.py:596
  15.1 11.8 %collective-permute-start.1 = (bf16[2,80,512]{2,1,0:T(8,128)(2,1)}, bf16[2,80,512]{2,1,0:T(8,128)(2,1)S(1)}, u32[]{:S(2)}, u32[]{:S(2)}) collective-permute-start(bf16[2,80,512]{2,1,0:T(8,128)(2,1)} %get-tuple-element.26), channel_id=1, source_target_pairs={{128,0},{256,128},{384,256},{129,1},{257,129},{385,257},{130,2},{2... | collective-permute-start | bytes 491528 | tf_op jit(solution)/shard_map/ppermute | solution.py:597
  17.0 29.5 %all-to-all-start = ((bf16[32,128,128]{2,1,0:T(8,128)(2,1)}), bf16[32,128,128]{2,1,0:T(8,128)(2,1)S(1)}, u32[]{:S(2)}, u32[]{:S(2)}) async-start(bf16[32,128,128]{2,1,0:T(8,128)(2,1)} %get-tuple-element.29), calls=%async_computation | async-start | bytes 2097152 | tf_op jit(solution)/shard_map/all_to_all | solution.py:598
  26.9 0.8 copy-start.4
  26.9 0.8 copy-start.6
  26.9 5.2 %copy-start.12 = (f32[8,49]{1,0:T(8,128)S(1)}, f32[8,49]{1,0:T(8,128)}, u32[]{:S(2)}) copy-start(f32[8,49]{1,0:T(8,128)} %param.12) | copy-start | bytes 4708
  26.9 14.2 %copy-start.8 = (f32[512]{0:T(512)S(1)}, f32[512]{0:T(512)}, u32[]{:S(2)}) copy-start(f32[512]{0:T(512)} %param.11) | copy-start | bytes 6148
  27.7 10.9 %collective-permute-start.2 = (bf16[416,512]{1,0:T(8,128)(2,1)S(1)}, bf16[416,512]{1,0:T(8,128)(2,1)S(1)}, u32[]{:S(2)}, u32[]{:S(2)}) collective-permute-start(bf16[416,512]{1,0:T(8,128)(2,1)S(1)} %get-tuple-element.27), channel_id=1, source_target_pairs={{0,32},{32,64},{64,96},{1,33},{33,65},{65,97},{2,34},{34,66},{66,9... | collective-permute-start | bytes 1277960 | tf_op jit(solution)/shard_map/ppermute | solution.py:603
  30.8 9.5 %collective-permute-start.3 = (bf16[416,512]{1,0:T(8,128)(2,1)S(1)}, bf16[416,512]{1,0:T(8,128)(2,1)S(1)}, u32[]{:S(2)}, u32[]{:S(2)}) collective-permute-start(bf16[416,512]{1,0:T(8,128)(2,1)S(1)} %get-tuple-element.28), channel_id=1, source_target_pairs={{32,0},{64,32},{96,64},{33,1},{65,33},{97,65},{34,2},{66,34},{98,6... | collective-permute-start | bytes 1277960 | tf_op jit(solution)/shard_map/ppermute | solution.py:604
  37.1 1.5 %copy-start.9 = (f32[10,512,128]{2,1,0:T(8,128)}, f32[10,512,128]{2,1,0:T(8,128)S(1)}, u32[]{:S(2)}) copy-start(f32[10,512,128]{2,1,0:T(8,128)S(1)} %get-tuple-element.30.tab) | copy-start | bytes 7864324
  40.4 0.8 copy-start
  41.1 1.0 copy-start.1
  42.1 0.9 copy-start.3
  43.1 0.9 copy-start.5
  44.0 0.9 copy-start.7
  46.5 1.7 %copy-start.10 = (f32[10,512,128]{2,1,0:T(8,128)S(1)}, f32[10,512,128]{2,1,0:T(8,128)}, u32[]{:S(2)}) copy-start(f32[10,512,128]{2,1,0:T(8,128)} %copy-done.9) | copy-start | bytes 7864324
  107.7 6.6 %collective-permute-start.4 = (bf16[64,128]{1,0:T(8,128)(2,1)S(1)}, bf16[64,128]{1,0:T(8,128)(2,1)S(1)}, u32[]{:S(2)}, u32[]{:S(2)}) collective-permute-start(bf16[64,128]{1,0:T(8,128)(2,1)S(1)} %get-tuple-element.34.mine), channel_id=1, source_target_pairs={{0,128},{128,0},{256,384},{384,256},{1,129},{129,1},{257,385},{385... | collective-permute-start | bytes 49160 | tf_op jit(solution)/shard_map/ppermute | solution.py:635

commit v3 on v2

--- a/solution.py
+++ b/solution.py
@@ -66,7 +66,8 @@
     return jax.ShapeDtypeStruct(dims, dtype)
 
 
-def pack_body(wq_in, wo_in, tok_in, grad_in, w_out, rows, down, up, wq, wo, sems):
+def pack_body(wq_in, wo_in, tok_in, grad_in, w_out, rows, near, far, wq, wo, sems):
+    even = lax.axis_index("gy") % 2 == 0
     copies = [
         pltpu.make_async_copy(wq_in, wq, sems.at[0]),
         pltpu.make_async_copy(wo_in, wo, sems.at[1]),
@@ -77,47 +78,76 @@
         copy.start()
     copies[0].wait()
     copies[1].wait()
-    parts = []
-    for c in range(2):
-        parts += [wq[:, (3 * c + j) * 128 : (3 * c + j + 1) * 128].astype(F32) for j in range(3)]
+
+    def half(c):
+        parts = [wq[:, (3 * c + j) * 128 : (3 * c + j + 1) * 128].astype(F32) for j in range(3)]
         parts += [wo[:, (2 * c + j) * 128 : (2 * c + j + 1) * 128].astype(F32) for j in range(2)]
-    block = jnp.concatenate(parts, axis=0).astype(BF)
-    for d in range(DP):
-        w_out[d] = block
+        block = jnp.concatenate(parts, axis=0).astype(BF)
+        for d in range(DP):
+            w_out[d] = block
+
+    pl.when(even)(lambda: half(0))
+    pl.when(jnp.logical_not(even))(lambda: half(1))
     copies[2].wait()
     copies[3].wait()
-    for s in range(CAP):
-        t, g = s * CELLS, ROWS + s * CELLS
-        down[s, 0:T_ROWS, :] = rows[t + CELLS - T_ROWS : t + CELLS, :]
-        down[s, T_ROWS:STRIP, :] = rows[g + CELLS - G_ROWS : g + CELLS, :]
-        up[s, 0:T_ROWS, :] = rows[t : t + T_ROWS, :]
-        up[s, T_ROWS:STRIP, :] = rows[g : g + G_ROWS, :]
-
-
-def corner_body(place, tiles, rows, above, below, to_right, to_left):
-    over = jnp.maximum(place[0] - 1, 0)
-    under = jnp.minimum(place[0] + 1, 3)
-    col = place[1]
-    for out, top, bottom in ((to_right, 15, 3), (to_left, 12, 0)):
-        out[0 : 2 * ROWS, :] = rows[...]
-        out[2 * ROWS : 2 * ROWS + STRIP, :] = above[
-            (tiles[over, col, 1] == top).astype(jnp.int32)
-        ]
-        out[2 * ROWS + STRIP : MESSAGE, :] = below[
-            (tiles[under, col, 1] == bottom).astype(jnp.int32)
-        ]
+
+    def strips(down, up):
+        for s in range(CAP):
+            t, g = s * CELLS, ROWS + s * CELLS
+            down[s, 0:T_ROWS, :] = rows[t + CELLS - T_ROWS : t + CELLS, :]
+            down[s, T_ROWS:STRIP, :] = rows[g + CELLS - G_ROWS : g + CELLS, :]
+            up[s, 0:T_ROWS, :] = rows[t : t + T_ROWS, :]
+            up[s, T_ROWS:STRIP, :] = rows[g : g + G_ROWS, :]
+
+    pl.when(even)(lambda: strips(near, far))
+    pl.when(jnp.logical_not(even))(lambda: strips(far, near))
+
+
+def corner_body(place, tiles, rows, near, far, first, second, local):
+    local[0 : 2 * ROWS, :] = rows[...]
+    row, col = place[0], place[1]
+    over = jnp.maximum(row - 1, 0)
+    under = jnp.minimum(row + 1, 3)
+
+    def build(above, below, to_right, to_left):
+        for n, strips in enumerate((above, below)):
+            for s in range(CAP):
+                at = 2 * ROWS + (2 * n + s) * STRIP
+                local[at : at + STRIP, :] = strips[s]
+        for out, top, bottom in ((to_right, 15, 3), (to_left, 12, 0)):
+            out[0 : 2 * ROWS, :] = rows[...]
+            out[2 * ROWS : 2 * ROWS + STRIP, :] = above[
+                (tiles[over, col, 1] == top).astype(jnp.int32)
+            ]
+            out[2 * ROWS + STRIP : MESSAGE, :] = below[
+                (tiles[under, col, 1] == bottom).astype(jnp.int32)
+            ]
+
+    for odd_row in range(2):
+        for odd_col in range(2):
+            here = ((row & 1) == odd_row) & ((col & 1) == odd_col)
+            rows_of = (near, far) if odd_row else (far, near)
+            outs = (second, first) if odd_col else (first, second)
+            pl.when(here)(functools.partial(build, *rows_of, *outs))
 
 
 def plan_tiles(place, tiles, plan, crow, ccol):
     my_row, my_col = place[0], place[1]
-    steps = [(0, 0)] * 2 + [(-1, 0)] * 2 + [(1, 0)] * 2 + [(0, -1)] * 2 + [(0, 1)] * 2
-    corners = [(-1, -1, 15), (-1, 1, 12), (1, -1, 3), (1, 1, 0)]
+    side = 1 - 2 * (my_col & 1)
+    steps = [(0, 0)] * 2 + [(-1, 0)] * 2 + [(1, 0)] * 2 + [(0, side)] * 2 + [(0, -side)] * 2
+    even = side > 0
+    corners = [
+        (-1, side, jnp.where(even, 12, 15)),
+        (-1, -side, jnp.where(even, 15, 12)),
+        (1, side, jnp.where(even, 0, 3)),
+        (1, -side, jnp.where(even, 3, 0)),
+    ]
     for t, (dy, dx, *corner) in enumerate(steps + corners):
         ry, rx = my_row + dy, my_col + dx
         there = (ry >= 0) & (ry < 4) & (rx >= 0) & (rx < 4)
         ty, tx = jnp.clip(ry, 0, 3), jnp.clip(rx, 0, 3)
         if corner:
-            tile = jnp.int32(corner[0])
+            tile = corner[0]
             there = there & ((tiles[ty, tx, 0] == tile) | (tiles[ty, tx, 1] == tile))
         else:
             tile = tiles[ty, tx, t % 2]
@@ -147,10 +177,10 @@
         return carry
 
     lax.fori_loop(0, TILES, tile_plan, 0)
-
-
-def table_body(place, tiles, base_ref, tab, plan, crow, ccol):
-    plan_tiles(place, tiles, plan, crow, ccol)
+    plan[0, 47] = my_row & 1
+
+
+def bias_tables(base_ref, tab):
     query = lax.broadcasted_iota(jnp.int32, (CELLS, 128), 0)
     lane = lax.broadcasted_iota(jnp.int32, (CELLS, 128), 1)
     key = lane & 63
@@ -177,7 +207,7 @@
     tab[FAR] = jnp.full((BROWS, 128), -jnp.inf, F32)
 
 
-def prep_body(rows, above, below, left, right, gain, out):
+def prepare(local, left, right, gain, out):
     normed = out.at[pl.ds(0, PAIRS * ROWS)]
     grads = out.at[pl.ds(PAIRS * ROWS, PAIRS * ROWS)]
     own = out.at[pl.ds(2 * PAIRS * ROWS, ROWS)]
@@ -188,21 +218,21 @@
         inv = lax.rsqrt(jnp.mean(x * x, axis=-1, keepdims=True) + 1e-06)
         return (x * inv * gain_row).astype(BF)
 
-    own[...] = rows[0:ROWS, :]
-    for t, source in ((0, rows), (6, left), (8, right)):
+    own[...] = local[0:ROWS, :]
+    for t, source in ((0, local), (6, left), (8, right)):
         at = t * CELLS
         normed[at : at + ROWS, :] = norm(source[0:ROWS, :])
         grads[at : at + ROWS, :] = source[ROWS : 2 * ROWS, :]
-    at_a, at_b = 2 * ROWS, 2 * ROWS + STRIP
+    at_a, at_b, at_c = 2 * ROWS, 2 * ROWS + STRIP, 2 * ROWS + 2 * STRIP
     upper = [
-        (2, above[0]),
-        (3, above[1]),
+        (2, local[at_a : at_a + STRIP, :]),
+        (3, local[at_b : at_b + STRIP, :]),
         (10, left[at_a : at_a + STRIP, :]),
         (11, right[at_a : at_a + STRIP, :]),
     ]
     lower = [
-        (4, below[0]),
-        (5, below[1]),
+        (4, local[at_c : at_c + STRIP, :]),
+        (5, local[at_c + STRIP : at_c + 2 * STRIP, :]),
         (12, left[at_b : at_b + STRIP, :]),
         (13, right[at_b : at_b + STRIP, :]),
     ]
@@ -222,10 +252,13 @@
 
 def main_body(
     plan,
-    packed,
-    weights,
+    local,
+    first,
+    second,
+    w_mine,
+    w_other,
     gain,
-    tab,
+    base,
     update,
     grad_tokens,
     sums,
@@ -250,27 +283,30 @@
     dv,
     hist,
     rowsum,
+    packed,
+    tab,
 ):
+    bias_tables(base, tab)
+    prepare(local, first, second, gain, packed)
     normed = packed.at[pl.ds(0, PAIRS * ROWS)]
     grads = packed.at[pl.ds(PAIRS * ROWS, PAIRS * ROWS)]
     tokens = packed.at[pl.ds(2 * PAIRS * ROWS, ROWS)]
-    for c in range(2):
+    core = plan[0, 47]
+    for c, part in ((core, w_mine), (1 - core, w_other)):
         for j in range(3):
-            at = WROWS * c + 16 * j
-            wq[:, (3 * c + j) * 128 : (3 * c + j + 1) * 128] = weights[
-                :, at : at + 16, :
-            ].reshape(D, 128)
-        both = weights[:, WROWS * c + 48 : WROWS * c + 64, :].astype(F32)
+            wq[3 * c + j] = part[:, 16 * j : 16 * j + 16, :].reshape(D, 128)
+        both = part[:, 48:64, :].astype(F32)
         for j in range(2):
-            wo[:, (2 * c + j) * 128 : (2 * c + j + 1) * 128] = (
-                both[:, 8 * j : 8 * j + 8, :].reshape(INNER, 128).astype(BF)
-            )
+            wo[2 * c + j] = both[:, 8 * j : 8 * j + 8, :].reshape(INNER, 128).astype(BF)
+
+    def columns(blocks, first, last):
+        return jnp.concatenate([blocks[j] for j in range(first, last)], axis=1)
 
     gain_row = gain[...]
     for j in range(3):
         cols = slice(j * INNER, (j + 1) * INNER)
-        qkv[:, cols] = dot(normed[...], wq[:, cols]).astype(BF)
-    gatt[...] = dot(grads[...], wo[...], NT).astype(BF)
+        qkv[:, cols] = dot(normed[...], columns(wq, 2 * j, 2 * j + 2)).astype(BF)
+    gatt[...] = dot(grads[...], columns(wo, 0, 4), NT).astype(BF)
 
     dk[...] = jnp.zeros_like(dk)
     dv[...] = jnp.zeros_like(dv)
@@ -418,7 +454,7 @@
 
     dqkv[:, INNER : 2 * INNER] = (dk[...] * SCALE).astype(BF)
     dqkv[:, 2 * INNER : 3 * INNER] = dv[...].astype(BF)
-    update[...] = dot(attended[...], wo[...]).astype(BF)
+    update[...] = dot(attended[...], columns(wo, 0, 4)).astype(BF)
     grad_out = dot(attended[...], grads[0:ROWS, :], TN)
     for c in range(2):
         pair = [
@@ -435,7 +471,7 @@
             for d in range(DP):
                 at = d * WROWS + (j % 3) * 16
                 sums[j // 3, at : at + 16, :] = block[d * 16 : (d + 1) * 16]
-    d_normed = dot(dqkv[...], wq[...], NT)
+    d_normed = dot(dqkv[...], columns(wq, 0, 6), NT)
     x = tokens[...].astype(F32)
     inv = lax.rsqrt(jnp.mean(x * x, axis=-1, keepdims=True) + 1e-06)
     scaled = d_normed * gain_row
@@ -533,7 +569,7 @@
     grad_bias[...] = out[:, 0:49]
 
 
-def layer(plan, packed, weights, gain, table):
+def layer(plan, local, first, second, w_mine, w_other, gain, base):
     f32 = lambda *dims: pltpu.VMEM(dims, F32)
     bf = lambda *dims: pltpu.VMEM(dims, BF)
     return call(
@@ -543,10 +579,10 @@
             shape((ROWS, D), BF),
             shape((2, DP * WROWS + SMALL, 128), BF),
         ],
-        [SM] + [VM] * 4,
+        [SM] + [VM] * 7,
         [
-            bf(D, 3 * INNER),
-            bf(INNER, D),
+            bf(6, D, 128),
+            bf(4, INNER, 128),
             bf(PAIRS * ROWS, 3 * INNER),
             bf(PAIRS * ROWS, INNER),
             bf(BROWS, INNER),
@@ -566,25 +602,27 @@
             f32(ROWS, INNER),
             f32(HEADS, 128),
             f32(CAP, HEADS, 128),
+            bf(2 * PAIRS * ROWS + ROWS, D),
+            f32(FAR + 1, BROWS, 128),
         ],
         limit=40,
         flops=4000000000,
         traffic=12000000,
-    )(plan, packed, weights, gain, table)
+    )(plan, local, first, second, w_mine, w_other, gain, base)
 
 
 def shards(tokens, tile_ids, w_qkv, w_out, norm_gain, rel_bias, update_grad):
     my_row = lax.axis_index("gy")
     my_col = lax.axis_index("gx")
     place = jnp.stack([my_row, my_col]).astype(jnp.int32)
-    forth = [(0, 1), (1, 2), (2, 3)]
-    back = [(1, 0), (2, 1), (3, 2)]
+    pairs = [(0, 1), (1, 0), (2, 3), (3, 2)]
+    middle = [(1, 2), (2, 1)]
 
     tiles = tile_ids.reshape(4, 4, CAP)
     strip = shape((CAP, STRIP, D), BF)
-    w_send, rows, down, up = call(
+    w_send, rows, near, far = call(
         pack_body,
-        [shape((DP, 2 * WROWS, 128), BF), shape((2 * ROWS, D), BF), strip, strip],
+        [shape((DP, WROWS, 128), BF), shape((2 * ROWS, D), BF), strip, strip],
         [HBM, HBM, HBM, HBM],
         [
             pltpu.VMEM((16, 3 * INNER), BF),
@@ -593,30 +631,32 @@
         ],
         limit=60,
     )(w_qkv, w_out, tokens.reshape(ROWS, D), update_grad.reshape(ROWS, D))
-    above = lax.ppermute(down, "gy", forth)
-    below = lax.ppermute(up, "gy", back)
-    weights = lax.all_to_all(w_send, "dp", 0, 0, tiled=True)
+    near = lax.ppermute(near, "gy", pairs)
+    far = lax.ppermute(far, "gy", middle)
+    w_mine = lax.all_to_all(w_send, "dp", 0, 0, tiled=True)
     message = shape((MESSAGE, D), BF)
-    to_right, to_left = call(corner_body, [message, message], [SM, SM, VM, VM, VM], flops=16000000000)(
-        place, tiles, rows, above, below
-    )
-    left = lax.ppermute(to_right, "gx", forth)
-    right = lax.ppermute(to_left, "gx", back)
+    stays = shape((2 * ROWS + 4 * STRIP, D), BF)
+    first, second, local = call(
+        corner_body, [message, message, stays], [SM, SM, VM, VM, VM], flops=16000000000
+    )(place, tiles, rows, near, far)
+    first = lax.ppermute(first, "gx", pairs)
+    second = lax.ppermute(second, "gx", middle)
     base = jnp.pad(rel_bias.reshape(HEADS, 7, 7), ((0, 0), (0, 0), (0, 1))).reshape(HEADS, 56)
     base = jnp.pad(base, ((0, 0), (0, 72)))
-    table, plan = pl.pallas_call(
-        table_body,
-        out_shape=[shape((10, BROWS, 128), F32), shape((TILES, 48), jnp.int32)],
-        in_specs=[SM, SM, VM],
-        out_specs=[VM, SM],
+    plan = pl.pallas_call(
+        plan_tiles,
+        out_shape=shape((TILES, 48), jnp.int32),
+        in_specs=[SM, SM],
+        out_specs=SM,
         scratch_shapes=[pltpu.SMEM((TILES,), jnp.int32), pltpu.SMEM((TILES,), jnp.int32)],
-        compiler_params=pltpu.CompilerParams(vmem_limit_bytes=16 * 2**20),
         cost_estimate=pl.CostEstimate(flops=2000000, bytes_accessed=4000000, transcendentals=0),
-    )(place, tiles, base)
-    packed = call(prep_body, shape((2 * PAIRS * ROWS + ROWS, D), BF), [VM] * 6)(
-        rows, above, below, left, right, norm_gain.reshape(1, D)
+    )(place, tiles)
+    w_mine = lax.optimization_barrier((w_mine, first, second, plan))[0]
+    w_other = lax.ppermute(w_mine, "gy", pairs)
+
+    update, grad_tokens, sums = layer(
+        plan, local, first, second, w_mine, w_other, norm_gain.reshape(1, D), base
     )
-    update, grad_tokens, sums = layer(plan, packed, weights, norm_gain.reshape(1, D), table)
 
     got = lax.all_to_all(sums, "gy", 0, 0, tiled=True, axis_index_groups=CORES)
     got = call(
@@ -632,7 +672,7 @@
     got = call(last_sum_body, shape((8, WROWS + SMALL, 128), BF), [VM])(got)
     got = lax.all_to_all(got, ("gy", "gx"), 0, 0, tiled=True, axis_index_groups=ZS)
     mine, small = call(z_body, [shape((WROWS, 128), BF), shape((8, 128), F32)], [VM])(got)
-    theirs = lax.ppermute(mine, "gy", [(0, 1), (1, 0), (2, 3), (3, 2)])
+    theirs = lax.ppermute(mine, "gy", pairs)
     grad_qkv, grad_out, grad_gain, grad_bias = call(
         finish_body,
         [

time: 116 us -> 108 us (0.931)
  local copies, waits for them, and re-layouts: 8.08 us -> 1 us
  blocking collectives: 53.5 us -> 50.9 us
  starting transfers between devices: 34 us -> 35.4 us
    unnamed x26 -> x16, local copies, waits for them, and re-layouts: 7.8 us -> 0.73 us
    all_to_all x1, blocking collectives: 19.6 us -> 15.5 us  [shards(): lax.all_to_all(got, ('gy', 'gx'), 0, 0, tiled=True, axis_index_groups=ZS)]
    all_to_all x1, blocking collectives: 16.2 us -> 18.1 us  [shards(): got = lax.all_to_all(got, 'dp', 0, 0, tiled=True, axis_index_groups=YS)]
    ppermute x5 -> x6, starting transfers between devices: 24.3 us -> 25.7 us  [the longest x1 8.92 us: shards(): near = lax.ppermute(near, 'gy', pairs)]
    pallas_call x4 -> x3, Pallas kernels: 8.13 us -> 7.07 us  [the longest x1 4.23 us: shards(): pl.pallas_call(plan_tiles, out_shape=shape((TILES, 48), jnp.int32), in_sp...]
    ppermute x5 -> x6, waiting for transfers between devices: 2.56 us -> 3.35 us  [the longest x1 1.7 us: shards(): w_other = lax.ppermute(w_mine, 'gy', pairs)]
  transfers between devices with their start and end apart: 6 -> 7, of which waited for: 3 -> 4; matrix products, arithmetic and copies ran while one was open for 0% -> 0% of each run, Pallas kernels for 5% -> 5%
where the time goes in v3:
time: 108 us
  blocking collectives  50.9 us (47%)
  starting transfers between devices  35.4 us (33%)
  Pallas kernels  14.5 us (13%)
  waiting for transfers between devices  4.8 us (4%)
    all_to_all x1, blocking collectives, shards(): got = lax.all_to_all(got, 'dp', 0, 0, tiled=True, axis_index_groups=YS)  18.1 us
    all_to_all x1, blocking collectives, shards(): lax.all_to_all(got, ('gy', 'gx'), 0, 0, tiled=True, axis_index_groups=ZS)  15.5 us
    all_to_all x1, blocking collectives, shards(): got = lax.all_to_all(got, 'dp', 0, 0, tiled=True, axis_index_groups=XS)  13 us
    all_to_all x1, starting transfers between devices, shards(): w_mine = lax.all_to_all(w_send, 'dp', 0, 0, tiled=True)  9.68 us
    ppermute x1, starting transfers between devices, shards(): near = lax.ppermute(near, 'gy', pairs)  8.92 us
    ppermute x1, starting transfers between devices, shards(): theirs = lax.ppermute(mine, 'gy', pairs)  5.96 us
    pallas_call x1, Pallas kernels, layer(): call(main_body, [shape((ROWS, D), BF), shape((ROWS, D), BF), shape((2, DP...  5.89 us
    ppermute x1, starting transfers between devices, shards(): far = lax.ppermute(far, 'gy', middle)  5.16 us
  transfers between devices with their start and end apart: 7, of which 4 were waited for; matrix products, arithmetic and copies ran while one was open for 0% of the time, Pallas kernels for 5%

profile of v3, /device:TPU:1, one launch (start us, length us, event | category | flops | bytes accessed | tf_op | source)
XLA Modules:
  0.0 107.6 jit_solution(2759852781883861761)
XLA Ops:
  0.6 0.0 copy-start.6
  0.6 2.1 %shard_map.119 = (bf16[32,64,128]{2,1,0:T(8,128)(2,1)}, bf16[256,512]{1,0:T(8,128)(2,1)}, bf16[2,80,512]{2,1,0:T(8,128)(2,1)}, bf16[2,80,512]{2,1,0:T(8,128)(2,1)}) custom-call(bf16[16,768]{1,0:T(8,128)(2,1)} %wq_in.1, bf16[8,512]{1,0:T(8,128)(2,1)} %wo_in.1, bf16[128,512]{1,0:T(8,128)(2,1)} %bitcast.10, bf16[128,512]{1,0:T(8,128)(2,1)} %bitcast.11), custom_call_target="tpu_custom_call" | custom-call | flops 1000000 | bytes 1000000 | tf_op jit(solution)/shard_map/pallas_call | solution.py:623
  2.7 0.0 copy-start.4
  2.7 8.9 %collective-permute-start = (bf16[2,80,512]{2,1,0:T(8,128)(2,1)}, bf16[2,80,512]{2,1,0:T(8,128)(2,1)S(1)}, u32[]{:S(2)}, u32[]{:S(2)}) collective-permute-start(bf16[2,80,512]{2,1,0:T(8,128)(2,1)} %get-tuple-element.24), channel_id=1, source_target_pairs={{0,128},{128,0},{256,384},{384,256},{1,129},{129,1},{257,385},{385... | collective-permute-start | bytes 491528 | tf_op jit(solution)/shard_map/ppermute | solution.py:634
  11.6 5.2 %collective-permute-start.1 = (bf16[2,80,512]{2,1,0:T(8,128)(2,1)}, bf16[2,80,512]{2,1,0:T(8,128)(2,1)S(1)}, u32[]{:S(2)}, u32[]{:S(2)}) collective-permute-start(bf16[2,80,512]{2,1,0:T(8,128)(2,1)} %get-tuple-element.25), channel_id=1, source_target_pairs={{128,256},{256,128},{129,257},{257,129},{130,258},{258,130},{131,2... | collective-permute-start | bytes 491528 | tf_op jit(solution)/shard_map/ppermute | solution.py:635
  16.8 9.7 %all-to-all-start = ((bf16[32,64,128]{2,1,0:T(8,128)(2,1)}), bf16[32,64,128]{2,1,0:T(8,128)(2,1)S(1)}, u32[]{:S(2)}, u32[]{:S(2)}) async-start(bf16[32,64,128]{2,1,0:T(8,128)(2,1)} %get-tuple-element.29), calls=%async_computation | async-start | bytes 1048576 | tf_op jit(solution)/shard_map/all_to_all | solution.py:636
  26.5 0.0 copy-done.6
  26.5 0.1 copy.17.tiles
  26.6 0.0 copy-start
  26.6 0.1 pad_add_fusion.place
  26.7 0.0 copy-start.2
  26.7 0.0 collective-permute-done.near
  26.7 0.0 collective-permute-done.1.far
  26.7 0.0 copy-done.4
  26.7 0.0 copy-start.7
  26.7 0.0 copy-start.5
  26.8 0.8 shard_map.120
  27.5 0.0 copy-done
  27.5 0.0 copy-done.2
  27.6 3.1 %collective-permute-start.2 = (bf16[416,512]{1,0:T(8,128)(2,1)S(1)}, bf16[416,512]{1,0:T(8,128)(2,1)S(1)}, u32[]{:S(2)}, u32[]{:S(2)}) collective-permute-start(bf16[416,512]{1,0:T(8,128)(2,1)S(1)} %get-tuple-element.27), channel_id=1, source_target_pairs={{0,32},{32,0},{64,96},{96,64},{1,33},{33,1},{65,97},{97,65},{2,34}... | collective-permute-start | bytes 1277960 | tf_op jit(solution)/shard_map/ppermute | solution.py:642
  30.7 0.7 collective-permute-start.3
  31.4 4.2 %shard_map.118.plan = s32[14,48]{1,0:T(8,128)} custom-call(s32[2]{0:T(128)} %copy-done.2, s32[4,4,2]{2,1,0:T(4,128)} %copy-done), custom_call_target="tpu_custom_call" | custom-call | flops 2000000 | bytes 4000000 | tf_op jit(solution)/shard_map/pallas_call | solution.py:646
  35.6 0.8 collective-permute-done.2.first
  36.4 0.0 collective-permute-done.3.second
  36.4 1.5 %all-to-all-done.w_mine = bf16[32,64,128]{2,1,0:T(8,128)(2,1)S(1)} async-done(((bf16[32,64,128]{2,1,0:T(8,128)(2,1)}), bf16[32,64,128]{2,1,0:T(8,128)(2,1)S(1)}, u32[]{:S(2)}, u32[]{:S(2)}) %all-to-all-start) | async-done | bytes 524320 | tf_op jit(solution)/shard_map/all_to_all | solution.py:636
  37.9 1.9 %collective-permute-start.4 = (bf16[32,64,128]{2,1,0:T(8,128)(2,1)S(1)}, bf16[32,64,128]{2,1,0:T(8,128)(2,1)S(1)}, u32[]{:S(2)}, u32[]{:S(2)}) collective-permute-start(bf16[32,64,128]{2,1,0:T(8,128)(2,1)S(1)} %all-to-all-done.w_mine), channel_id=1, source_target_pairs={{0,128},{128,0},{256,384},{384,256},{1,129},{129,1},{257,385},{385... | collective-permute-start | bytes 1572872 | tf_op jit(solution)/shard_map/ppermute | solution.py:655
  39.8 0.0 copy-done.7
  39.8 0.1 reshape.43
  39.9 0.1 reshape.44
  40.0 1.7 %collective-permute-done.4.w_other = bf16[32,64,128]{2,1,0:T(8,128)(2,1)S(1)} collective-permute-done((bf16[32,64,128]{2,1,0:T(8,128)(2,1)S(1)}, bf16[32,64,128]{2,1,0:T(8,128)(2,1)S(1)}, u32[]{:S(2)}, u32[]{:S(2)}) %collective-permute-start.4) | collective-permute-done | bytes 524320 | tf_op jit(solution)/shard_map/ppermute | solution.py:655
  41.7 0.0 copy-done.5
  41.7 0.0 copy-start.1
  41.7 0.7 copy-done.1
  42.4 5.9 %shard_map.121 = (bf16[128,512]{1,0:T(8,128)(2,1)}, bf16[128,512]{1,0:T(8,128)(2,1)}, bf16[2,2064,128]{2,1,0:T(8,128)(2,1)S(1)}) custom-call(s32[14,48]{1,0:T(8,128)S(1)} %copy-done.1, bf16[576,512]{1,0:T(8,128)(2,1)S(1)} %get-tuple-element.26.local, bf16[416,512]{1,0:T(8,128)(2,1)S(1)} %collective-permute-done.2.first, ...), custom_call_target="tpu_custom_call" | custom-call | flops 4000000000 | bytes 12000000 | tf_op jit(solution)/shard_map/pallas_call | solution.py:575
  48.3 4.3 %all_to_all.25.received = bf16[2,2064,128]{2,1,0:T(8,128)(2,1)S(1)} all-to-all(bf16[2,2064,128]{2,1,0:T(8,128)(2,1)S(1)} %get-tuple-element.33), channel_id=1, replica_groups={{0,128},{256,384},{1,129},{257,385},{2,130},{258,386},{3,131},{259,387}..., dimensions={0} | all-to-all | bytes 2113536 | tf_op jit(solution)/shard_map/all_to_all | solution.py:661
  52.6 0.1 shard_map.122
  52.7 13.0 %all_to_all.26.received = bf16[4,528,128]{2,1,0:T(8,128)(2,1)S(1)} all-to-all(bf16[4,528,128]{2,1,0:T(8,128)(2,1)S(1)} %shard_map.122), channel_id=1, replica_groups={{0,8,16,24},{1,9,17,25},{2,10,18,26},{3,11,19,27},{4,12,20,28},{5,13,21..., dimensions={0} | all-to-all | bytes 1081344 | tf_op jit(solution)/shard_map/all_to_all | solution.py:667
  65.7 0.0 copy-start.3
  65.7 0.1 shard_map.123
  65.8 18.1 %all_to_all.27.received = bf16[8,80,128]{2,1,0:T(8,128)(2,1)S(1)} all-to-all(bf16[8,80,128]{2,1,0:T(8,128)(2,1)S(1)} %shard_map.123), channel_id=1, replica_groups={{0,1,2,3,4,5,6,7},{8,9,10,11,12,13,14,15},{16,17,18,19,20,21,22,23},{24..., dimensions={0} | all-to-all | bytes 327680 | tf_op jit(solution)/shard_map/all_to_all | solution.py:671
  83.9 15.5 %all_to_all.28.received = bf16[8,80,128]{2,1,0:T(8,128)(2,1)S(1)} all-to-all(bf16[8,80,128]{2,1,0:T(8,128)(2,1)S(1)} %shard_map.124), channel_id=1, replica_groups={{0,32,64,96,256,288,320,352},{128,160,192,224,384,416,448,480},{1,33,65..., dimensions={0} | all-to-all | bytes 327680 | tf_op jit(solution)/shard_map/all_to_all | solution.py:673
  99.5 6.0 %collective-permute-start.5 = (bf16[64,128]{1,0:T(8,128)(2,1)S(1)}, bf16[64,128]{1,0:T(8,128)(2,1)S(1)}, u32[]{:S(2)}, u32[]{:S(2)}) collective-permute-start(bf16[64,128]{1,0:T(8,128)(2,1)S(1)} %get-tuple-element.34.mine), channel_id=1, source_target_pairs={{0,128},{128,0},{256,384},{384,256},{1,129},{129,1},{257,385},{385... | collective-permute-start | bytes 49160 | tf_op jit(solution)/shard_map/ppermute | solution.py:675
  105.4 0.8 collective-permute-done.5.theirs
  106.3 0.0 copy-done.3
  106.3 1.3 %shard_map.126 = (f32[16,768]{1,0:T(8,128)}, f32[8,512]{1,0:T(8,128)}, f32[1,512]{1,0:T(1,128)}, f32[8,49]{1,0:T(8,128)}) custom-call(s32[2]{0:T(128)S(1)} %copy-done.3, bf16[64,128]{1,0:T(8,128)(2,1)S(1)} %get-tuple-element.34.mine, bf16[64,128]{1,0:T(8,128)(2,1)S(1)} %collective-permute-done.5.theirs, f32[8,128]{1,0:T(8,128)S(1)} %get-tuple-element.35.small_in), custom_call_target="tpu_custom_call" | custom-call | flops 1000000 | bytes 1000000 | tf_op jit(solution)/shard_map/pallas_call | solution.py:676
  (4 shorter events, 0.1 us)
Async XLA Ops:
  0.6 25.9 %copy-start.6 = (s32[1,4,4,2]{2,3,1,0:T(2,128)S(1)}, s32[1,4,4,2]{2,3,1,0:T(2,128)}, u32[]{:S(2)}) copy-start(s32[1,4,4,2]{2,3,1,0:T(2,128)} %param.8) | copy-start | bytes 388
  2.7 24.0 %copy-start.4 = (bf16[256,512]{1,0:T(8,128)(2,1)S(1)}, bf16[256,512]{1,0:T(8,128)(2,1)}, u32[]{:S(2)}) copy-start(bf16[256,512]{1,0:T(8,128)(2,1)} %get-tuple-element.23.rows) | copy-start | bytes 786436
  2.7 24.0 %collective-permute-start = (bf16[2,80,512]{2,1,0:T(8,128)(2,1)}, bf16[2,80,512]{2,1,0:T(8,128)(2,1)S(1)}, u32[]{:S(2)}, u32[]{:S(2)}) collective-permute-start(bf16[2,80,512]{2,1,0:T(8,128)(2,1)} %get-tuple-element.24), channel_id=1, source_target_pairs={{0,128},{128,0},{256,384},{384,256},{1,129},{129,1},{257,385},{385... | collective-permute-start | bytes 491528 | tf_op jit(solution)/shard_map/ppermute | solution.py:634
  11.6 15.1 %collective-permute-start.1 = (bf16[2,80,512]{2,1,0:T(8,128)(2,1)}, bf16[2,80,512]{2,1,0:T(8,128)(2,1)S(1)}, u32[]{:S(2)}, u32[]{:S(2)}) collective-permute-start(bf16[2,80,512]{2,1,0:T(8,128)(2,1)} %get-tuple-element.25), channel_id=1, source_target_pairs={{128,256},{256,128},{129,257},{257,129},{130,258},{258,130},{131,2... | collective-permute-start | bytes 491528 | tf_op jit(solution)/shard_map/ppermute | solution.py:635
  16.8 21.1 %all-to-all-start = ((bf16[32,64,128]{2,1,0:T(8,128)(2,1)}), bf16[32,64,128]{2,1,0:T(8,128)(2,1)S(1)}, u32[]{:S(2)}, u32[]{:S(2)}) async-start(bf16[32,64,128]{2,1,0:T(8,128)(2,1)} %get-tuple-element.29), calls=%async_computation | async-start | bytes 1048576 | tf_op jit(solution)/shard_map/all_to_all | solution.py:636
  26.6 0.9 copy-start
  26.7 0.8 copy-start.2
  26.7 13.1 %copy-start.7 = (f32[8,49]{1,0:T(8,128)S(1)}, f32[8,49]{1,0:T(8,128)}, u32[]{:S(2)}) copy-start(f32[8,49]{1,0:T(8,128)} %param.12) | copy-start | bytes 4708
  26.7 14.9 %copy-start.5 = (f32[512]{0:T(512)S(1)}, f32[512]{0:T(512)}, u32[]{:S(2)}) copy-start(f32[512]{0:T(512)} %param.11) | copy-start | bytes 6148
  27.6 8.9 %collective-permute-start.2 = (bf16[416,512]{1,0:T(8,128)(2,1)S(1)}, bf16[416,512]{1,0:T(8,128)(2,1)S(1)}, u32[]{:S(2)}, u32[]{:S(2)}) collective-permute-start(bf16[416,512]{1,0:T(8,128)(2,1)S(1)} %get-tuple-element.27), channel_id=1, source_target_pairs={{0,32},{32,0},{64,96},{96,64},{1,33},{33,1},{65,97},{97,65},{2,34}... | collective-permute-start | bytes 1277960 | tf_op jit(solution)/shard_map/ppermute | solution.py:642
  30.7 5.8 %collective-permute-start.3 = (bf16[416,512]{1,0:T(8,128)(2,1)S(1)}, bf16[416,512]{1,0:T(8,128)(2,1)S(1)}, u32[]{:S(2)}, u32[]{:S(2)}) collective-permute-start(bf16[416,512]{1,0:T(8,128)(2,1)S(1)} %get-tuple-element.28), channel_id=1, source_target_pairs={{32,64},{64,32},{33,65},{65,33},{34,66},{66,34},{35,67},{67,35},{3... | collective-permute-start | bytes 1277960 | tf_op jit(solution)/shard_map/ppermute | solution.py:643
  37.9 3.8 %collective-permute-start.4 = (bf16[32,64,128]{2,1,0:T(8,128)(2,1)S(1)}, bf16[32,64,128]{2,1,0:T(8,128)(2,1)S(1)}, u32[]{:S(2)}, u32[]{:S(2)}) collective-permute-start(bf16[32,64,128]{2,1,0:T(8,128)(2,1)S(1)} %all-to-all-done.w_mine), channel_id=1, source_target_pairs={{0,128},{128,0},{256,384},{384,256},{1,129},{129,1},{257,385},{385... | collective-permute-start | bytes 1572872 | tf_op jit(solution)/shard_map/ppermute | solution.py:655
  41.7 0.7 copy-start.1
  65.7 40.5 %copy-start.3 = (s32[2]{0:T(128)S(1)}, s32[2]{0:T(128)}, u32[]{:S(2)}) copy-start(s32[2]{0:T(128)} %copy-done.2) | copy-start | bytes 28
  99.5 6.8 %collective-permute-start.5 = (bf16[64,128]{1,0:T(8,128)(2,1)S(1)}, bf16[64,128]{1,0:T(8,128)(2,1)S(1)}, u32[]{:S(2)}, u32[]{:S(2)}) collective-permute-start(bf16[64,128]{1,0:T(8,128)(2,1)S(1)} %get-tuple-element.34.mine), channel_id=1, source_target_pairs={{0,128},{128,0},{256,384},{384,256},{1,129},{129,1},{257,385},{385... | collective-permute-start | bytes 49160 | tf_op jit(solution)/shard_map/ppermute | solution.py:675
